TPU v7x, 32 devices: a whole 2x2x4 slice. The times are simulated.
32 devices in a mesh: dp: 32 (over z, y, x, core).
Axes of the slice: x: 2, y: 2, z: 4, core: 2. Of those that a mesh axis runs over, the one named last changes fastest.
Arguments:
- tokens: bfloat16 [8192, 1024], P('dp'), may hold values from -6 to 6
- memory: bfloat16 [65536, 1024], P('dp'), may hold values from -6 to 6
- target_lengths: int32 [32], P('dp'), may hold values from 128 to 256, as said below
- memory_lengths: int32 [32], P('dp'), may hold values from 1024 to 2048, as said below
- cotangent: bfloat16 [8192, 1024], P('dp'), may hold values from -6 to 6
- self_query: bfloat16 [1024, 1024], P('dp'), may hold values from -0.1875 to 0.1875
- self_key: bfloat16 [1024, 1024], P('dp'), may hold values from -0.1875 to 0.1875
- self_value: bfloat16 [1024, 1024], P('dp'), may hold values from -0.1875 to 0.1875
- self_output: bfloat16 [1024, 1024], P('dp'), may hold values from -0.75 to 0.75
- first_gain: bfloat16 [1024], P('dp'), may hold values from 0.5 to 1.5
- first_shift: bfloat16 [1024], P('dp'), may hold values from -3 to 3
- cross_query: bfloat16 [1024, 1024], P('dp'), may hold values from -0.1875 to 0.1875
- cross_key: bfloat16 [1024, 1024], P('dp'), may hold values from -0.1875 to 0.1875
- cross_value: bfloat16 [1024, 1024], P('dp'), may hold values from -0.1875 to 0.1875
- cross_output: bfloat16 [1024, 1024], P('dp'), may hold values from -1.5 to 1.5
- second_gain: bfloat16 [1024], P('dp'), may hold values from 0.5 to 1.5
- second_shift: bfloat16 [1024], P('dp'), may hold values from -3 to 3
- inner_weight: bfloat16 [1024, 4096], P('dp'), may hold values from -0.1875 to 0.1875
- outer_weight: bfloat16 [4096, 1024], P('dp'), may hold values from -0.09375 to 0.09375
- third_gain: bfloat16 [1024], P('dp'), may hold values from 0.5 to 1.5
- third_shift: bfloat16 [1024], P('dp'), may hold values from -3 to 3
Outputs:
- output: bfloat16 [8192, 1024], P('dp')
- tokens_grad: float32 [8192, 1024], P('dp')
- memory_grad: float32 [65536, 1024], P('dp')
- grad_self_query: float32 [1024, 1024], P('dp')
- grad_self_key: float32 [1024, 1024], P('dp')
- grad_self_value: float32 [1024, 1024], P('dp')
- grad_self_output: float32 [1024, 1024], P('dp')
- grad_first_gain: float32 [1024], P('dp')
- grad_first_shift: float32 [1024], P('dp')
- grad_cross_query: float32 [1024, 1024], P('dp')
- grad_cross_key: float32 [1024, 1024], P('dp')
- grad_cross_value: float32 [1024, 1024], P('dp')
- grad_cross_output: float32 [1024, 1024], P('dp')
- grad_second_gain: float32 [1024], P('dp')
- grad_second_shift: float32 [1024], P('dp')
- grad_inner_weight: float32 [1024, 4096], P('dp')
- grad_outer_weight: float32 [4096, 1024], P('dp')
- grad_third_gain: float32 [1024], P('dp')
- grad_third_shift: float32 [1024], P('dp')
Inputs may be any that keep to these rules, and one draw needn't show every extreme that they name: `target_lengths`: some question has exactly 256 live target tokens. `memory_lengths`: some question has exactly 2048 live memory tokens.
All inputs are finite; a program needn't handle non-finite values.
Results may differ from a plain program's by a relative error of at most 0.02.
The roundings to bfloat16 on the way count: a program that leaves them out, or rounds other values in their place, can miss the bound.
Values may be sent and summed in bfloat16 or wider, within the bound.
A program may use at most 256 MiB of HBM per device.

v0:
```python
import math

import jax
import jax.numpy as jnp
from jax import lax
from jax.sharding import PartitionSpec as P

HEAD = 64
TGT = 256
MEM = 2048


def matmul(operand, factor):
    return jnp.dot(operand, factor, preferred_element_type=jnp.float32)


def dot_left(operand, factor):
    return lax.dot_general(
        operand, factor, (((0,), (0,)), ((), ())), preferred_element_type=jnp.float32
    )


def dot_right(operand, factor):
    return lax.dot_general(
        operand, factor, (((1,), (1,)), ((), ())), preferred_element_type=jnp.float32
    )


def layer_norm(summed, norm_gain, norm_shift):
    average = jnp.mean(summed, axis=-1, keepdims=True)
    centred = summed - average
    spread = jnp.mean(centred * centred, axis=-1, keepdims=True)
    return centred * lax.rsqrt(spread + 1e-05) * norm_gain + norm_shift


def exact_gelu(inner_pre):
    return jax.nn.gelu(inner_pre, approximate=False)


def flatten_rows(matrix):
    return matrix.reshape(-1, 128)


def split_heads(rows_in):
    return rows_in.reshape(rows_in.shape[0], rows_in.shape[1] // HEAD, HEAD)


def masked_scores(query_heads, key_heads, allowed):
    scores = jnp.einsum("qhd,khd->hqk", query_heads, key_heads, preferred_element_type=jnp.float32)
    scores = scores * (1.0 / math.sqrt(HEAD))
    return jnp.where(allowed[None], scores, -1e30)


def self_allowed(length):
    positions = jnp.arange(TGT)
    return (positions[None, :] <= positions[:, None]) & (positions[None, :] < length)


def cross_allowed(length):
    return jnp.broadcast_to(jnp.arange(MEM)[None, :] < length, (TGT, MEM))


def attend_forward(query_rows, key_rows, value_rows, allowed):
    scores = masked_scores(split_heads(query_rows), split_heads(key_rows), allowed)
    row_peak = jnp.max(scores, axis=-1, keepdims=True)
    raised = jnp.exp(scores - row_peak)
    row_total = jnp.sum(raised, axis=-1, keepdims=True)
    prob_rows = (raised / row_total).astype(jnp.bfloat16)
    mixture = jnp.einsum(
        "hqk,khd->qhd", prob_rows, split_heads(value_rows), preferred_element_type=jnp.float32
    )
    return (mixture.reshape(query_rows.shape).astype(jnp.bfloat16), row_peak + jnp.log(row_total))


def attend_backward(query_rows, key_rows, value_rows, allowed, log_total, grad_mixture):
    query_heads = split_heads(query_rows)
    key_heads = split_heads(key_rows)
    value_heads = split_heads(value_rows)
    grad_heads = split_heads(grad_mixture)
    prob_rows = jnp.exp(masked_scores(query_heads, key_heads, allowed) - log_total)
    grad_values = jnp.einsum(
        "hqk,qhd->khd",
        prob_rows.astype(jnp.bfloat16),
        grad_heads,
        preferred_element_type=jnp.float32,
    )
    grad_probs = jnp.einsum(
        "qhd,khd->hqk", grad_heads, value_heads, preferred_element_type=jnp.float32
    )
    inner_sum = jnp.sum(prob_rows * grad_probs, axis=-1, keepdims=True)
    grad_scores = (prob_rows * (grad_probs - inner_sum)).astype(jnp.bfloat16)
    score_scale = 1.0 / math.sqrt(HEAD)
    grad_queries = (
        jnp.einsum("hqk,khd->qhd", grad_scores, key_heads, preferred_element_type=jnp.float32)
        * score_scale
    )
    grad_keys = (
        jnp.einsum("hqk,qhd->khd", grad_scores, query_heads, preferred_element_type=jnp.float32)
        * score_scale
    )
    return (
        grad_queries.reshape(query_rows.shape).astype(jnp.bfloat16),
        grad_keys.reshape(key_rows.shape).astype(jnp.bfloat16),
        grad_values.reshape(value_rows.shape).astype(jnp.bfloat16),
    )


def self_forward(pieces):
    query_rows, key_rows, value_rows, length = pieces
    return attend_forward(query_rows, key_rows, value_rows, self_allowed(length))


def cross_forward(pieces):
    query_rows, key_rows, value_rows, length = pieces
    return attend_forward(query_rows, key_rows, value_rows, cross_allowed(length))


def self_backward(pieces):
    query_rows, key_rows, value_rows, length, log_total, grad_rows = pieces
    return attend_backward(
        query_rows, key_rows, value_rows, self_allowed(length), log_total, grad_rows
    )


def cross_backward(pieces):
    query_rows, key_rows, value_rows, length, log_total, grad_rows = pieces
    return attend_backward(
        query_rows, key_rows, value_rows, cross_allowed(length), log_total, grad_rows
    )


def on_device(
    tokens,
    memory,
    target_lengths,
    memory_lengths,
    cotangent,
    self_query,
    self_key,
    self_value,
    self_output,
    first_gain,
    first_shift,
    cross_query,
    cross_key,
    cross_value,
    cross_output,
    second_gain,
    second_shift,
    inner_weight,
    outer_weight,
    third_gain,
    third_shift,
):
    questions = target_lengths.shape[0]
    width = tokens.shape[1]
    hidden_width = inner_weight.shape[1]

    def by_question(rows_in, per_question):
        return rows_in.reshape(questions, per_question, width)

    query_full, key_full, value_full, output_full, gain_one, shift_one = (
        lax.all_gather(self_query, "dp", axis=0, tiled=True),
        lax.all_gather(self_key, "dp", axis=0, tiled=True),
        lax.all_gather(self_value, "dp", axis=0, tiled=True),
        lax.all_gather(self_output, "dp", axis=0, tiled=True),
        lax.all_gather(first_gain, "dp", axis=0, tiled=True),
        lax.all_gather(first_shift, "dp", axis=0, tiled=True),
    )
    queries = matmul(tokens, query_full).astype(jnp.bfloat16)
    key_rows = matmul(tokens, key_full).astype(jnp.bfloat16)
    value_rows = matmul(tokens, value_full).astype(jnp.bfloat16)
    self_mixture, self_totals = lax.map(
        self_forward,
        (
            by_question(queries, TGT),
            by_question(key_rows, TGT),
            by_question(value_rows, TGT),
            target_lengths,
        ),
    )
    self_mixture = self_mixture.reshape(tokens.shape)
    first_sum = tokens.astype(jnp.float32) + matmul(self_mixture, output_full)
    first_out = layer_norm(first_sum, gain_one.astype(jnp.float32), shift_one.astype(jnp.float32))
    first_low = first_out.astype(jnp.bfloat16)
    cquery_full, ckey_full, cvalue_full, coutput_full, gain_two, shift_two = (
        lax.all_gather(cross_query, "dp", axis=0, tiled=True),
        lax.all_gather(cross_key, "dp", axis=0, tiled=True),
        lax.all_gather(cross_value, "dp", axis=0, tiled=True),
        lax.all_gather(cross_output, "dp", axis=0, tiled=True),
        lax.all_gather(second_gain, "dp", axis=0, tiled=True),
        lax.all_gather(second_shift, "dp", axis=0, tiled=True),
    )
    cross_queries = matmul(first_low, cquery_full).astype(jnp.bfloat16)
    cross_keys = matmul(memory, ckey_full).astype(jnp.bfloat16)
    cross_values = matmul(memory, cvalue_full).astype(jnp.bfloat16)
    cross_mixture, cross_totals = lax.map(
        cross_forward,
        (
            by_question(cross_queries, TGT),
            by_question(cross_keys, MEM),
            by_question(cross_values, MEM),
            memory_lengths,
        ),
    )
    cross_mixture = cross_mixture.reshape(tokens.shape)
    second_sum = first_out + matmul(cross_mixture, coutput_full)
    second = layer_norm(second_sum, gain_two.astype(jnp.float32), shift_two.astype(jnp.float32))
    second_low = second.astype(jnp.bfloat16)
    inner_full, outer_full, gain_three, shift_three = (
        lax.all_gather(inner_weight, "dp", axis=0, tiled=True),
        lax.all_gather(outer_weight, "dp", axis=0, tiled=True),
        lax.all_gather(third_gain, "dp", axis=0, tiled=True),
        lax.all_gather(third_shift, "dp", axis=0, tiled=True),
    )
    inner_pre = matmul(second_low, inner_full)
    activated = exact_gelu(inner_pre).astype(jnp.bfloat16)
    third_sum = second + matmul(activated, outer_full)
    output_rows = layer_norm(
        third_sum, gain_three.astype(jnp.float32), shift_three.astype(jnp.float32)
    )
    inner_full, outer_full, gain_three, shift_three = (
        lax.all_gather(inner_weight, "dp", axis=0, tiled=True),
        lax.all_gather(outer_weight, "dp", axis=0, tiled=True),
        lax.all_gather(third_gain, "dp", axis=0, tiled=True),
        lax.all_gather(third_shift, "dp", axis=0, tiled=True),
    )
    _, third_pull = jax.vjp(
        layer_norm, third_sum, gain_three.astype(jnp.float32), shift_three.astype(jnp.float32)
    )
    grad_third_sum, grad_third_gain, grad_third_shift = third_pull(cotangent.astype(jnp.float32))
    grad_outer_in = grad_third_sum.astype(jnp.bfloat16)
    grad_outer_weight = dot_left(activated, grad_outer_in)
    grad_activated = dot_right(grad_outer_in, outer_full)
    _, gelu_pull = jax.vjp(exact_gelu, inner_pre)
    grad_inner = gelu_pull(grad_activated)[0].astype(jnp.bfloat16)
    grad_inner_weight = dot_left(second_low, grad_inner)
    grad_second = grad_third_sum + dot_right(grad_inner, inner_full)
    ffn_owned = (
        lax.psum_scatter(flatten_rows(grad_inner_weight), "dp", scatter_dimension=0, tiled=True),
        lax.psum_scatter(flatten_rows(grad_outer_weight), "dp", scatter_dimension=0, tiled=True),
        lax.psum_scatter(grad_third_gain, "dp", scatter_dimension=0, tiled=True),
        lax.psum_scatter(grad_third_shift, "dp", scatter_dimension=0, tiled=True),
    )
    cquery_full, ckey_full, cvalue_full, coutput_full, gain_two, shift_two = (
        lax.all_gather(cross_query, "dp", axis=0, tiled=True),
        lax.all_gather(cross_key, "dp", axis=0, tiled=True),
        lax.all_gather(cross_value, "dp", axis=0, tiled=True),
        lax.all_gather(cross_output, "dp", axis=0, tiled=True),
        lax.all_gather(second_gain, "dp", axis=0, tiled=True),
        lax.all_gather(second_shift, "dp", axis=0, tiled=True),
    )
    _, second_pull = jax.vjp(
        layer_norm, second_sum, gain_two.astype(jnp.float32), shift_two.astype(jnp.float32)
    )
    grad_second_sum, grad_second_gain, grad_second_shift = second_pull(grad_second)
    grad_cross_in = grad_second_sum.astype(jnp.bfloat16)
    grad_cross_output = dot_left(cross_mixture, grad_cross_in)
    grad_cross_mixture = dot_right(grad_cross_in, coutput_full).astype(jnp.bfloat16)
    grad_cq, grad_ck, grad_cv = lax.map(
        cross_backward,
        (
            by_question(cross_queries, TGT),
            by_question(cross_keys, MEM),
            by_question(cross_values, MEM),
            memory_lengths,
            cross_totals,
            by_question(grad_cross_mixture, TGT),
        ),
    )
    grad_cq = grad_cq.reshape(tokens.shape)
    grad_ck = grad_ck.reshape(memory.shape)
    grad_cv = grad_cv.reshape(memory.shape)
    grad_cross_query = dot_left(first_low, grad_cq)
    grad_cross_key = dot_left(memory, grad_ck)
    grad_cross_value = dot_left(memory, grad_cv)
    memory_grad = dot_right(grad_ck, ckey_full) + dot_right(grad_cv, cvalue_full)
    grad_first = grad_second_sum + dot_right(grad_cq, cquery_full)
    cross_owned = (
        lax.psum_scatter(flatten_rows(grad_cross_query), "dp", scatter_dimension=0, tiled=True),
        lax.psum_scatter(flatten_rows(grad_cross_key), "dp", scatter_dimension=0, tiled=True),
        lax.psum_scatter(flatten_rows(grad_cross_value), "dp", scatter_dimension=0, tiled=True),
        lax.psum_scatter(flatten_rows(grad_cross_output), "dp", scatter_dimension=0, tiled=True),
        lax.psum_scatter(grad_second_gain, "dp", scatter_dimension=0, tiled=True),
        lax.psum_scatter(grad_second_shift, "dp", scatter_dimension=0, tiled=True),
    )
    query_full, key_full, value_full, output_full, gain_one, shift_one = (
        lax.all_gather(self_query, "dp", axis=0, tiled=True),
        lax.all_gather(self_key, "dp", axis=0, tiled=True),
        lax.all_gather(self_value, "dp", axis=0, tiled=True),
        lax.all_gather(self_output, "dp", axis=0, tiled=True),
        lax.all_gather(first_gain, "dp", axis=0, tiled=True),
        lax.all_gather(first_shift, "dp", axis=0, tiled=True),
    )
    _, first_pull = jax.vjp(
        layer_norm, first_sum, gain_one.astype(jnp.float32), shift_one.astype(jnp.float32)
    )
    grad_first_sum, grad_first_gain, grad_first_shift = first_pull(grad_first)
    grad_self_in = grad_first_sum.astype(jnp.bfloat16)
    grad_self_output = dot_left(self_mixture, grad_self_in)
    grad_self_mixture = dot_right(grad_self_in, output_full).astype(jnp.bfloat16)
    grad_queries, grad_keys, grad_values = lax.map(
        self_backward,
        (
            by_question(queries, TGT),
            by_question(key_rows, TGT),
            by_question(value_rows, TGT),
            target_lengths,
            self_totals,
            by_question(grad_self_mixture, TGT),
        ),
    )
    grad_queries = grad_queries.reshape(tokens.shape)
    grad_keys = grad_keys.reshape(tokens.shape)
    grad_values = grad_values.reshape(tokens.shape)
    grad_self_query = dot_left(tokens, grad_queries)
    grad_self_key = dot_left(tokens, grad_keys)
    grad_self_value = dot_left(tokens, grad_values)
    tokens_grad = (
        grad_first_sum
        + dot_right(grad_queries, query_full)
        + dot_right(grad_keys, key_full)
        + dot_right(grad_values, value_full)
    )
    self_owned = (
        lax.psum_scatter(flatten_rows(grad_self_query), "dp", scatter_dimension=0, tiled=True),
        lax.psum_scatter(flatten_rows(grad_self_key), "dp", scatter_dimension=0, tiled=True),
        lax.psum_scatter(flatten_rows(grad_self_value), "dp", scatter_dimension=0, tiled=True),
        lax.psum_scatter(flatten_rows(grad_self_output), "dp", scatter_dimension=0, tiled=True),
        lax.psum_scatter(grad_first_gain, "dp", scatter_dimension=0, tiled=True),
        lax.psum_scatter(grad_first_shift, "dp", scatter_dimension=0, tiled=True),
    )
    owned = self_owned + cross_owned + ffn_owned
    return (
        output_rows.astype(jnp.bfloat16),
        tokens_grad,
        memory_grad,
        owned[0].reshape(-1, width),
        owned[1].reshape(-1, width),
        owned[2].reshape(-1, width),
        owned[3].reshape(-1, width),
        owned[4],
        owned[5],
        owned[6].reshape(-1, width),
        owned[7].reshape(-1, width),
        owned[8].reshape(-1, width),
        owned[9].reshape(-1, width),
        owned[10],
        owned[11],
        owned[12].reshape(-1, hidden_width),
        owned[13].reshape(-1, width),
        owned[14],
        owned[15],
    )


def solution(mesh):
    placed = (
        P("dp", None),
        P("dp", None),
        P("dp"),
        P("dp"),
        P("dp", None),
        P("dp", None),
        P("dp", None),
        P("dp", None),
        P("dp", None),
        P("dp"),
        P("dp"),
        P("dp", None),
        P("dp", None),
        P("dp", None),
        P("dp", None),
        P("dp"),
        P("dp"),
        P("dp", None),
        P("dp", None),
        P("dp"),
        P("dp"),
    )
    return jax.shard_map(
        on_device,
        mesh=mesh,
        in_specs=placed,
        out_specs=(
            P("dp", None),
            P("dp", None),
            P("dp", None),
            P("dp", None),
            P("dp", None),
            P("dp", None),
            P("dp", None),
            P("dp"),
            P("dp"),
            P("dp", None),
            P("dp", None),
            P("dp", None),
            P("dp", None),
            P("dp"),
            P("dp"),
            P("dp", None),
            P("dp", None),
            P("dp"),
            P("dp"),
        ),
        check_vma=False,
    )
```

profile of v0, /device:TPU:14, one launch (start us, length us, event | category | flops | bytes accessed | tf_op | source)
XLA Modules:
  0.0 2231.0 jit_solution(12240790866621753802)
XLA Ops:
  19.8 41.1 %all-reduce.13 = (bf16[1024]{0:T(1024)(128)(2,1)S(1)}, bf16[1024]{0:T(1024)(128)(2,1)S(1)}, bf16[1024]{0:T(1024)(128)(2,1)S(1)}, bf16[1024]{0:T(1024)(128)(2,1)S...) all-reduce(bf16[1024]{0:T(1024)(128)(2,1)S(1)} %dynamic-update-slice, ...), channel_id=1, replica_groups=mesh['dp'=32] {'dp'}, use_global_device_ids=true, to_apply=%add.1 | all-reduce | flops 6144 | bytes 24576
  61.7 5.3 all-gather.13.cloned.1.call-done
  69.7 55.8 %all-gather.15.cloned.1.call-done = bf16[1024,1024]{1,0:T(8,128)(2,1)} async-done(((bf16[32,1024]{1,0:T(8,128)(2,1)}), bf16[1024,1024]{1,0:T(8,128)(2,1)}) %all-gather.15.cloned.1.call-update) | async-done | bytes 2097168 | tf_op jit(solution)/shard_map/all_gather | solution.py:164
  128.0 55.6 %all-gather.11.cloned.1.call-done = bf16[1024,1024]{1,0:T(8,128)(2,1)} async-done(((bf16[32,1024]{1,0:T(8,128)(2,1)}), bf16[1024,1024]{1,0:T(8,128)(2,1)}) %all-gather.11.cloned.1.call-update) | async-done | bytes 2097168 | tf_op jit(solution)/shard_map/all_gather | solution.py:165
  189.9 51.7 %all-gather.17.cloned.1.call-done = bf16[1024,1024]{1,0:T(8,128)(2,1)} async-done(((bf16[32,1024]{1,0:T(8,128)(2,1)}), bf16[1024,1024]{1,0:T(8,128)(2,1)}) %all-gather.17.cloned.1.call-update) | async-done | bytes 2097168 | tf_op jit(solution)/shard_map/all_gather | solution.py:166
  244.3 55.3 %all-gather.21.cloned.1.call-done = bf16[1024,1024]{1,0:T(8,128)(2,1)} async-done(((bf16[32,1024]{1,0:T(8,128)(2,1)}), bf16[1024,1024]{1,0:T(8,128)(2,1)}) %all-gather.21.cloned.1.call-update) | async-done | bytes 2097168 | tf_op jit(solution)/shard_map/all_gather | solution.py:187
  302.1 55.4 %all-gather.23.cloned.1.call-done = bf16[1024,1024]{1,0:T(8,128)(2,1)} async-done(((bf16[32,1024]{1,0:T(8,128)(2,1)}), bf16[1024,1024]{1,0:T(8,128)(2,1)}) %all-gather.23.cloned.1.call-update) | async-done | bytes 2097168 | tf_op jit(solution)/shard_map/all_gather | solution.py:188
  357.5 9.4 convolution_convert_fusion
  366.9 48.7 %all-gather.19.cloned.1.call-done = bf16[1024,1024]{1,0:T(8,128)(2,1)} async-done(((bf16[32,1024]{1,0:T(8,128)(2,1)}), bf16[1024,1024]{1,0:T(8,128)(2,1)}) %all-gather.19.cloned.1.call-update) | async-done | bytes 2097168 | tf_op jit(solution)/shard_map/all_gather | solution.py:189
  415.6 10.0 convolution_convert_fusion.1
  425.7 13.3 fusion.56
  439.0 13.6 fusion
  452.6 15.3 fusion.28
  467.9 5.9 all-gather.25.cloned.1.call-done
  476.5 77.2 %all-gather.27.cloned.1.call-done = bf16[1024,4096]{1,0:T(8,128)(2,1)} async-done(((bf16[32,4096]{1,0:T(8,128)(2,1)}), bf16[1024,4096]{1,0:T(8,128)(2,1)}) %all-gather.27.cloned.1.call-update) | async-done | bytes 8388624 | tf_op jit(solution)/shard_map/all_gather | solution.py:211
  553.7 15.9 multiply_convert_fusion.3
  569.6 62.9 %all-gather.29.cloned.1.call-done = bf16[4096,1024]{1,0:T(8,128)(2,1)} async-done(((bf16[128,1024]{1,0:T(8,128)(2,1)}), bf16[4096,1024]{1,0:T(8,128)(2,1)}) %all-gather.29.cloned.1.call-update) | async-done | bytes 8388624 | tf_op jit(solution)/shard_map/all_gather | solution.py:212
  632.5 6.5 fusion.58
  641.6 11.2 add_convert_fusion
  652.8 7.5 multiply_reduce_fusion.2
  661.7 23.7 %multiply_reduce_fusion = (f32[16,256]{1,0:T(8,128)S(1)}, f32[16,256,2048]{2,1,0:T(8,128)}) fusion(f32[16,256,2048]{2,1,0:T(8,128)} %get-tuple-element.156, f32[16,256]{1,0:T(8,128)S(1)} %log_add_fusion.1, bf16[256,16,64]{0,2,1:T(8,128)(2,1)S(1)} %bitcast.130, bf16[2048,16,64]{0,2,1:T(8,128)(2,1)} %bitcast.123), kind=kOutput, calls=%fused_computation.1 | convolution fusion | flops 1098903552 | bytes 71860224 | tf_op jit(solution)/shard_map/while/body/eval_jaxpr/qhd,khd->hqk/dot_general | solution.py:87
  685.4 28.2 %multiply_convert_fusion = bf16[16,256,2048]{2,1,0:T(8,128)(2,1)} fusion(f32[16,256,2048]{2,1,0:T(8,128)} %get-tuple-element.164, f32[16,256,2048]{2,1,0:T(8,128)} %get-tuple-element.156, f32[16,256]{1,0:T(8,128)S(1)} %get-tuple-element.163, f32[16,256]{1,0:T(8,128)S(1)} %log_add_fusion.1), kind=kLoop, calls=%fused_computation | loop fusion | flops 33554432 | bytes 83918848 | tf_op jit(solution)/shard_map/while/body/eval_jaxpr/convert_element_type | solution.py:91
  713.6 12.2 fusion.21
  725.9 2.9 multiply_reduce_fusion.3
  729.3 2.8 fusion.42
  732.1 4.9 reshape.396
  738.2 3.8 fusion.41
  742.0 5.0 reshape.404
  748.1 2.9 fusion.47
  751.0 4.9 reshape.398
  757.0 15.7 fusion.12
  772.7 10.0 convolution_bitcast_fusion
  782.7 5.4 copy.85
  788.1 4.9 reshape.402
  794.0 9.0 multiply_convert_fusion.1
  805.0 6.1 convolution_bitcast_fusion.1
  811.1 5.4 copy.84
  816.6 4.9 reshape.400
  824.8 3.0 fusion.22
  827.8 2.7 convolution_bitcast_fusion.2
  830.6 5.4 copy.83
  836.0 5.0 reshape.394
  842.0 3.4 multiply_reduce_fusion.1
  848.1 2.7 convolution_bitcast_fusion.3
  850.8 5.4 copy.82
  856.2 4.9 reshape.392
  863.5 3.7 convolution_bitcast_fusion.4
  867.3 5.4 copy.81
  872.6 4.9 reshape.390
  878.8 9.8 fusion.43
  888.6 18.0 reshape.406
  907.9 9.7 fusion.39
  917.6 18.0 reshape.408
  936.4 40.8 %all-reduce.12 = (f32[1024]{0:T(1024)S(1)}, f32[1024]{0:T(1024)S(1)}, f32[1024]{0:T(1024)S(1)}, f32[1024]{0:T(1024)S(1)}, f32[1024]{0:T(1024)S(1)}, /*index=5*/f32[1024]{0:T(1024)S(1)}) all-reduce(f32[1024]{0:T(1024)S(1)} %get-tuple-element.103, f32[1024]{0:T(1024)S(1)} %get-tuple-element.118, ...), channel_id=6, replica_groups=mesh['dp'=32] {'dp'}, use_global_device_ids=true, to_apply=%region_23.24.clone | all-reduce | flops 6144 | bytes 49152
  986.5 4.7 fusion.59
  991.3 7.3 convolution_add_fusion
  1001.8 121.6 %reduce-scatter.19.cloned.1.call-done = f32[256,128]{1,0:T(8,128)} async-done(((f32[8192,128]{1,0:T(8,128)}), f32[256,128]{1,0:T(8,128)}) %reduce-scatter.19.cloned.1.call-update) | async-done | bytes 131088 | tf_op jit(solution)/shard_map/reduce_scatter | solution.py:280
  1125.0 137.9 %reduce-scatter.23.cloned.1.call-done = f32[256,128]{1,0:T(8,128)} async-done(((f32[8192,128]{1,0:T(8,128)}), f32[256,128]{1,0:T(8,128)}) %reduce-scatter.23.cloned.1.call-update) | async-done | bytes 131088 | tf_op jit(solution)/shard_map/reduce_scatter | solution.py:282
  1264.5 137.5 %reduce-scatter.21.cloned.1.call-done = f32[256,128]{1,0:T(8,128)} async-done(((f32[8192,128]{1,0:T(8,128)}), f32[256,128]{1,0:T(8,128)}) %reduce-scatter.21.cloned.1.call-update) | async-done | bytes 131088 | tf_op jit(solution)/shard_map/reduce_scatter | solution.py:281
  1403.7 138.0 %reduce-scatter.15.cloned.1.call-done = f32[256,128]{1,0:T(8,128)} async-done(((f32[8192,128]{1,0:T(8,128)}), f32[256,128]{1,0:T(8,128)}) %reduce-scatter.15.cloned.1.call-update) | async-done | bytes 131088 | tf_op jit(solution)/shard_map/reduce_scatter | solution.py:328
  1543.3 137.3 %reduce-scatter.13.cloned.1.call-done = f32[256,128]{1,0:T(8,128)} async-done(((f32[8192,128]{1,0:T(8,128)}), f32[256,128]{1,0:T(8,128)}) %reduce-scatter.13.cloned.1.call-update) | async-done | bytes 131088 | tf_op jit(solution)/shard_map/reduce_scatter | solution.py:327
  1682.1 137.7 %reduce-scatter.11.cloned.1.call-done = f32[256,128]{1,0:T(8,128)} async-done(((f32[8192,128]{1,0:T(8,128)}), f32[256,128]{1,0:T(8,128)}) %reduce-scatter.11.cloned.1.call-update) | async-done | bytes 131088 | tf_op jit(solution)/shard_map/reduce_scatter | solution.py:326
  1821.4 213.8 %reduce-scatter.27.cloned.1.call-done = f32[1024,128]{1,0:T(8,128)} async-done(((f32[32768,128]{1,0:T(8,128)}), f32[1024,128]{1,0:T(8,128)}) %reduce-scatter.27.cloned.1.call-update) | async-done | bytes 524304 | tf_op jit(solution)/shard_map/reduce_scatter | solution.py:240
  2037.1 184.7 %reduce-scatter.29.cloned.1.call-done = f32[1024,128]{1,0:T(8,128)} async-done(((f32[32768,128]{1,0:T(8,128)}), f32[1024,128]{1,0:T(8,128)}) %reduce-scatter.29.cloned.1.call-update) | async-done | bytes 524304 | tf_op jit(solution)/shard_map/reduce_scatter | solution.py:241
  (251 shorter events, 80.1 us)
Async XLA Ops:
  7.2 118.3 %copy-start.7 = (bf16[256,1024]{1,0:T(8,128)(2,1)S(1)}, bf16[256,1024]{1,0:T(8,128)(2,1)}, u32[]{:S(2)}) copy-start(bf16[256,1024]{1,0:T(8,128)(2,1)} %param.21) | copy-start | bytes 1572868
  7.2 59.8 %all-gather.13.cloned.1.call-start = ((), (), s32[]{:S(2)}) async-start(), calls=%async_computation.11 | async-start | bytes 2162688 | tf_op jit(solution)/shard_map/all_gather | solution.py:163
  7.9 117.6 %all-gather.15.cloned.1.call-start = ((), (), s32[]{:S(2)}) async-start(), calls=%async_computation.12 | async-start | bytes 2162688 | tf_op jit(solution)/shard_map/all_gather | solution.py:164
  8.7 174.9 %all-gather.11.cloned.1.call-start = ((), (), s32[]{:S(2)}) async-start(), calls=%async_computation.10 | async-start | bytes 2162688 | tf_op jit(solution)/shard_map/all_gather | solution.py:165
  9.4 232.2 %all-gather.17.cloned.1.call-start = ((), (), s32[]{:S(2)}) async-start(), calls=%async_computation.13 | async-start | bytes 2162688 | tf_op jit(solution)/shard_map/all_gather | solution.py:166
  10.0 289.6 %all-gather.21.cloned.1.call-start = ((), (), s32[]{:S(2)}) async-start(), calls=%async_computation.15 | async-start | bytes 2162688 | tf_op jit(solution)/shard_map/all_gather | solution.py:187
  10.6 346.9 %all-gather.23.cloned.1.call-start = ((), (), s32[]{:S(2)}) async-start(), calls=%async_computation.16 | async-start | bytes 2162688 | tf_op jit(solution)/shard_map/all_gather | solution.py:188
  11.2 404.5 %all-gather.19.cloned.1.call-start = ((), (), s32[]{:S(2)}) async-start(), calls=%async_computation.14 | async-start | bytes 2162688 | tf_op jit(solution)/shard_map/all_gather | solution.py:189
  11.9 461.8 %all-gather.25.cloned.1.call-start = ((), (), s32[]{:S(2)}) async-start(), calls=%async_computation.17 | async-start | bytes 2162688 | tf_op jit(solution)/shard_map/all_gather | solution.py:190
  12.7 541.0 %all-gather.27.cloned.1.call-start = ((), (), s32[]{:S(2)}) async-start(), calls=%async_computation.18 | async-start | bytes 8650752 | tf_op jit(solution)/shard_map/all_gather | solution.py:211
  13.4 619.1 %all-gather.29.cloned.1.call-start = ((), (), s32[]{:S(2)}) async-start(), calls=%async_computation.19 | async-start | bytes 8650752 | tf_op jit(solution)/shard_map/all_gather | solution.py:212
  14.0 984.7 %reduce-scatter.17.cloned.1.call-start = ((), (), s32[]{:S(2)}) async-start(), calls=%async_computation.23 | async-start | bytes 4325376 | tf_op jit(solution)/shard_map/reduce_scatter | solution.py:329
  61.6 598.7 %copy-start.40 = (f32[1024]{0:T(1024)}, f32[1024]{0:T(1024)S(1)}, u32[]{:S(2)}) copy-start(f32[1024]{0:T(1024)S(1)} %convert_element_type.197) | copy-start | bytes 12292
  61.6 570.8 %copy-start.42 = (f32[1024]{0:T(1024)}, f32[1024]{0:T(1024)S(1)}, u32[]{:S(2)}) copy-start(f32[1024]{0:T(1024)S(1)} %convert_element_type.198) | copy-start | bytes 12292
  69.7 116.5 %copy-start.23 = (bf16[256,1024]{0,1:T(8,128)(2,1)}, bf16[256,1024]{0,1:T(8,128)(2,1)S(1)}, u32[]{:S(2)}) copy-start(bf16[256,1024]{0,1:T(8,128)(2,1)S(1)} %copy.72) | copy-start | bytes 1572868
  128.0 59.0 %copy-start.22 = (bf16[256,1024]{0,1:T(8,128)(2,1)}, bf16[256,1024]{0,1:T(8,128)(2,1)S(1)}, u32[]{:S(2)}) copy-start(bf16[256,1024]{0,1:T(8,128)(2,1)S(1)} %copy.73) | copy-start | bytes 1572868
  186.1 1.5 copy-start.32
  187.0 2.0 copy-start
  187.0 2.8 copy-start.44
  187.6 2.2 copy-start.46
  189.9 112.0 %copy-start.30 = (bf16[16,64,256]{2,1,0:T(8,128)(2,1)}, bf16[16,64,256]{2,1,0:T(8,128)(2,1)S(1)}, u32[]{:S(2)}) copy-start(bf16[16,64,256]{2,1,0:T(8,128)(2,1)S(1)} %fusion.27) | copy-start | bytes 1572868
  244.3 122.7 %copy-start.54 = (f32[256]{0:T(256)}, f32[256]{0:T(256)S(1)}, u32[]{:S(2)}) copy-start(f32[256]{0:T(256)S(1)} %multiply_reduce_fusion.8) | copy-start | bytes 3076
  302.1 123.5 %copy-start.10 = (bf16[256,1024]{0,1:T(8,128)(2,1)}, bf16[256,1024]{0,1:T(8,128)(2,1)S(1)}, u32[]{:S(2)}) copy-start(bf16[256,1024]{0,1:T(8,128)(2,1)S(1)} %copy.75) | copy-start | bytes 1572868
  415.6 10.0 copy-start.2
  467.9 101.7 %copy-start.38 = (bf16[16,64,256]{2,1,0:T(8,128)(2,1)}, bf16[16,64,256]{2,1,0:T(8,128)(2,1)S(1)}, u32[]{:S(2)}) copy-start(bf16[16,64,256]{2,1,0:T(8,128)(2,1)S(1)} %fusion.28) | copy-start | bytes 1572868
  476.2 184.1 %copy-start.3 = (f32[256,1024]{1,0:T(8,128)}, f32[256,1024]{1,0:T(8,128)S(1)}, u32[]{:S(2)}) copy-start(f32[256,1024]{1,0:T(8,128)S(1)} %get-tuple-element.158) | copy-start | bytes 3145732
  476.2 184.1 %copy-start.48 = (f32[256]{0:T(256)}, f32[256]{0:T(256)S(1)}, u32[]{:S(2)}) copy-start(f32[256]{0:T(256)S(1)} %broadcast_multiply_fusion.1) | copy-start | bytes 3076
  476.5 183.8 %copy-start.50 = (f32[256]{0:T(256)}, f32[256]{0:T(256)S(1)}, u32[]{:S(2)}) copy-start(f32[256]{0:T(256)S(1)} %fusion.37) | copy-start | bytes 3076
  632.5 6.8 copy-start.37
  639.0 2.6 copy-start.63
  641.5 11.2 copy-start.28
  641.6 11.2 copy-start.58
  652.8 7.5 copy-start.39
  652.8 7.9 copy-start.36
  660.7 65.1 %copy-start.5 = (f32[256,1024]{1,0:T(8,128)}, f32[256,1024]{1,0:T(8,128)S(1)}, u32[]{:S(2)}) copy-start(f32[256,1024]{1,0:T(8,128)S(1)} %get-tuple-element.145) | copy-start | bytes 3145732
  661.7 23.7 %copy-start.20 = (bf16[256,1024]{0,1:T(8,128)(2,1)}, bf16[256,1024]{0,1:T(8,128)(2,1)S(1)}, u32[]{:S(2)}) copy-start(bf16[256,1024]{0,1:T(8,128)(2,1)S(1)} %copy.76) | copy-start | bytes 1572868
  725.8 3.4 copy-start.25
  725.8 3.0 copy-start.55
  725.9 3.4 copy-start.31
  737.0 263.2 %reduce-scatter.25.cloned.1.call-start = ((), (), s32[]{:S(2)}) async-start(), calls=%async_computation.27 | async-start | bytes 4325376 | tf_op jit(solution)/shard_map/reduce_scatter | solution.py:283
  747.1 376.3 %reduce-scatter.19.cloned.1.call-start = ((), (), s32[]{:S(2)}) async-start(), calls=%async_computation.24 | async-start | bytes 4325376 | tf_op jit(solution)/shard_map/reduce_scatter | solution.py:280
  755.9 507.0 %reduce-scatter.23.cloned.1.call-start = ((), (), s32[]{:S(2)}) async-start(), calls=%async_computation.26 | async-start | bytes 4325376 | tf_op jit(solution)/shard_map/reduce_scatter | solution.py:282
  793.0 609.1 %reduce-scatter.21.cloned.1.call-start = ((), (), s32[]{:S(2)}) async-start(), calls=%async_computation.25 | async-start | bytes 4325376 | tf_op jit(solution)/shard_map/reduce_scatter | solution.py:281
  794.0 11.0 copy-start.60
  803.0 2.0 copy-start.12
  821.5 720.2 %reduce-scatter.15.cloned.1.call-start = ((), (), s32[]{:S(2)}) async-start(), calls=%async_computation.22 | async-start | bytes 4325376 | tf_op jit(solution)/shard_map/reduce_scatter | solution.py:328
  822.2 5.6 copy-start.8
  827.8 2.7 copy-start.14
  841.0 839.6 %reduce-scatter.13.cloned.1.call-start = ((), (), s32[]{:S(2)}) async-start(), calls=%async_computation.21 | async-start | bytes 4325376 | tf_op jit(solution)/shard_map/reduce_scatter | solution.py:327
  842.0 3.5 copy-start.1
  845.5 2.6 copy-start.9
  861.1 958.6 %reduce-scatter.11.cloned.1.call-start = ((), (), s32[]{:S(2)}) async-start(), calls=%async_computation.20 | async-start | bytes 4325376 | tf_op jit(solution)/shard_map/reduce_scatter | solution.py:326
  877.6 1157.5 %reduce-scatter.27.cloned.1.call-start = ((), (), s32[]{:S(2)}) async-start(), calls=%async_computation.28 | async-start | bytes 17301504 | tf_op jit(solution)/shard_map/reduce_scatter | solution.py:240
  906.6 1.2 copy-start.59
  906.7 1315.1 %reduce-scatter.29.cloned.1.call-start = ((), (), s32[]{:S(2)}) async-start(), calls=%async_computation.29 | async-start | bytes 17301504 | tf_op jit(solution)/shard_map/reduce_scatter | solution.py:241
  935.7 45.1 %copy-start.19 = (bf16[16,64,256]{2,1,0:T(8,128)(2,1)S(1)}, bf16[16,64,256]{2,1,0:T(8,128)(2,1)}, u32[]{:S(2)}) copy-start(bf16[16,64,256]{2,1,0:T(8,128)(2,1)} %copy-done.18) | copy-start | bytes 1572868
  935.7 47.5 %copy-start.17 = (bf16[16,64,256]{2,1,0:T(8,128)(2,1)S(1)}, bf16[16,64,256]{2,1,0:T(8,128)(2,1)}, u32[]{:S(2)}) copy-start(bf16[16,64,256]{2,1,0:T(8,128)(2,1)} %copy-done.16) | copy-start | bytes 1572868
  977.2 6.0 copy-start.34
  980.7 3.4 copy-start.15
  980.7 3.4 copy-start.35
  983.3 2.6 copy-start.13
  983.3 3.3 copy-start.61
  986.5 4.7 copy-start.27
  986.5 4.8 copy-start.62
  (20 other events, 19.7 us)
Sparse Core Ops, SparseCore 0:
  10.9 56.0 all-gather.12
  69.8 55.6 all-gather.14
  128.4 55.2 all-gather.10
  186.3 55.2 all-gather.16
  244.3 55.2 all-gather.20
  302.3 55.2 all-gather.22
  360.4 55.2 all-gather.18
  418.5 55.2 all-gather.24
  476.6 76.9 all-gather.26
  556.4 76.0 all-gather.28
  737.1 107.7 reduce-scatter.16
  847.1 137.0 reduce-scatter.24
  986.4 136.9 reduce-scatter.18
  1125.5 137.3 reduce-scatter.22
  1265.1 136.9 reduce-scatter.20
  1404.2 137.4 reduce-scatter.14
  1543.8 136.6 reduce-scatter.12
  1682.7 137.0 reduce-scatter.10
  1822.1 213.0 reduce-scatter.26
  2037.3 184.4 reduce-scatter.28
where the time goes:
time: 2240 us; the launch traced here: 2230 us
  waiting for transfers between devices  1690 us (75%)
  matrix products  252 us (11%)
  local copies, waits for them, and re-layouts  143 us (6%)
  blocking collectives  81.9 us (4%)
  other arithmetic  47.4 us (2%)
    reduce_scatter x1, waiting for transfers between devices, on_device(): lax.psum_scatter(flatten_rows(grad_inner_weight), 'dp', scatter_dimension...  214 us
    reduce_scatter x1, waiting for transfers between devices, on_device(): lax.psum_scatter(flatten_rows(grad_outer_weight), 'dp', scatter_dimension...  185 us
    reduce_scatter x1, waiting for transfers between devices, on_device(): lax.psum_scatter(flatten_rows(grad_self_value), 'dp', scatter_dimension=0...  138 us
    reduce_scatter x1, waiting for transfers between devices, on_device(): lax.psum_scatter(flatten_rows(grad_cross_value), 'dp', scatter_dimension=...  138 us
    reduce_scatter x1, waiting for transfers between devices, on_device(): lax.psum_scatter(flatten_rows(grad_self_query), 'dp', scatter_dimension=0...  138 us
    reduce_scatter x1, waiting for transfers between devices, on_device(): lax.psum_scatter(flatten_rows(grad_cross_key), 'dp', scatter_dimension=0,...  138 us
    reduce_scatter x1, waiting for transfers between devices, on_device(): lax.psum_scatter(flatten_rows(grad_self_key), 'dp', scatter_dimension=0,...  137 us
    reduce_scatter x1, waiting for transfers between devices, on_device(): lax.psum_scatter(flatten_rows(grad_cross_query), 'dp', scatter_dimension=...  122 us
  transfers between devices with their start and end apart: 20, of which 18 were waited for; matrix products, arithmetic and copies ran while one was open for 14% of the time, Pallas kernels for 0%

commit v1 on v0

v1 whole, which is shorter than its diff:
```python
import functools
import math

import jax
import jax.numpy as jnp
from jax import lax
from jax.experimental import pallas as pl
from jax.experimental.pallas import tpu as pltpu
from jax.sharding import PartitionSpec as P

HEAD = 64
EPS = 1e-05
SCALE = 1.0 / math.sqrt(HEAD)
LOG2E = 1.4426950408889634
BLOCKS = 32
MIB = 1024 * 1024
F32 = jnp.float32
BF16 = jnp.bfloat16


def nn(a, b):
    return jnp.dot(a, b, preferred_element_type=F32)


def nt(a, b):
    return lax.dot_general(a, b, (((1,), (1,)), ((), ())), preferred_element_type=F32)


def tn(a, b):
    return lax.dot_general(a, b, (((0,), (0,)), ((), ())), preferred_element_type=F32)


def whole(ref):
    return ref[...].reshape(-1, ref.shape[-1])


def call(body, name, out, grid=(), ins=None, outs=None, scratch=(), prefetch=0, limit=56, flops=0, moved=0):
    return pl.pallas_call(
        body,
        out_shape=out,
        grid_spec=pltpu.PrefetchScalarGridSpec(
            num_scalar_prefetch=prefetch,
            grid=grid,
            in_specs=ins,
            out_specs=outs,
            scratch_shapes=scratch,
        ),
        compiler_params=pltpu.CompilerParams(vmem_limit_bytes=limit * MIB),
        cost_estimate=pl.CostEstimate(flops=flops, bytes_accessed=moved, transcendentals=0),
        name=name,
    )


def full(shape):
    return pl.BlockSpec(shape, lambda *_: (0,) * len(shape))


def weight(at):
    return pl.BlockSpec((BLOCKS, 32, 1024), lambda *_: (0, at, 0))


def shape(dims, dtype):
    return jax.ShapeDtypeStruct(dims, dtype)


def norm_parts(summed):
    average = jnp.mean(summed, axis=-1, keepdims=True)
    centred = summed - average
    spread = jnp.mean(centred * centred, axis=-1, keepdims=True)
    scale = lax.rsqrt(spread + EPS)
    return centred * scale, scale


def norm_back(summed, gain, upstream):
    normal, scale = norm_parts(summed)
    grad_gain = jnp.sum(upstream * normal, axis=0, keepdims=True)
    grad_shift = jnp.sum(upstream, axis=0, keepdims=True)
    scaled = upstream * gain
    first = jnp.mean(scaled, axis=-1, keepdims=True)
    second = jnp.mean(scaled * normal, axis=-1, keepdims=True)
    return scale * (scaled - first - normal * second), grad_gain, grad_shift


def lanes(rows):
    return lax.broadcasted_iota(jnp.int32, (rows, 128), 1)


def stack_pair(rows):
    low = lanes(rows.shape[0]) < HEAD
    zero = jnp.zeros_like(rows)
    return jnp.concatenate([jnp.where(low, rows, zero), jnp.where(low, zero, rows)], axis=0)


def unstack_pair(stacked):
    half = stacked.shape[0] // 2
    return jnp.where(lanes(half) < HEAD, stacked[:half], stacked[half:])


def pair_forward(stacked, keys, values, mask):
    scores = nt(stacked, keys)
    if mask is not None:
        scores = mask(scores)
    peak = jnp.max(scores, axis=-1, keepdims=True)
    raised = jnp.exp2((scores - peak) * (SCALE * LOG2E))
    total = jnp.sum(raised, axis=-1, keepdims=True)
    mixed = nn(raised.astype(BF16), values) / total
    return mixed, peak * SCALE + jnp.log(total)


def pair_tile_back(q2, g2, keys, values, totals, inner, mask):
    scores = nt(keys, q2)
    probs = jnp.exp2(scores * (SCALE * LOG2E) - totals)
    if mask is not None:
        probs = mask(probs)
    grad_probs = nt(values, g2)
    grad_scores = (probs * (grad_probs - inner)).astype(BF16)
    grad_values = nn(probs.astype(BF16), g2)
    grad_keys = nn(grad_scores, q2) * SCALE
    grad_queries = tn(keys, grad_scores)
    return grad_queries, grad_keys, grad_values


def pair_inner(mixture, grad):
    product = mixture.astype(F32) * grad.astype(F32)
    half = jnp.where(
        (lax.broadcasted_iota(jnp.int32, (8, 128), 1) // HEAD)
        == lax.broadcasted_iota(jnp.int32, (8, 128), 0),
        1.0,
        0.0,
    ).astype(F32)
    sums = lax.dot_general(
        half, product, (((1,), (1,)), ((), ())),
        preferred_element_type=F32, precision=lax.Precision.HIGHEST,
    )
    return jnp.concatenate([sums[0:1], sums[1:2]], axis=1)


def join_grad_queries(grad):
    count = grad.shape[1] // 2
    joined = jnp.concatenate([grad[:HEAD, :count], grad[HEAD:, count:]], axis=0) * SCALE
    return joined.T.astype(BF16)


def kv_body(memory, wk, wv, keys, values):
    rows = memory[...]
    keys[...] = nn(rows, whole(wk)).astype(BF16)
    values[...] = nn(rows, whole(wv)).astype(BF16)


def kv_project(memory, stack, at_k, at_v):
    count, width = memory.shape
    tile = 512
    spec = pl.BlockSpec((tile, width), lambda i: (i, 0))
    return call(
        kv_body, "cross_kv", [shape(memory.shape, BF16)] * 2, (count // tile,),
        [spec, weight(at_k), weight(at_v)], [spec, spec],
        flops=4 * count * width * width, moved=12 * MIB + 4 * MIB,
    )(memory, stack, stack)


def self_body(length, tokens, wq, wk, wv, wo, wcq, vecs, q_o, k_o, v_o, mix_o, sum_o, first_o, low_o, cq_o, lse_o):
    rows = tokens[...]
    count, width = rows.shape
    q_o[...] = nn(rows, whole(wq)).astype(BF16)
    k_o[...] = nn(rows, whole(wk)).astype(BF16)
    v_o[...] = nn(rows, whole(wv)).astype(BF16)
    live = length[0]
    at_q = lax.rem(lax.broadcasted_iota(jnp.int32, (2 * count, count), 0), count)
    at_k = lax.broadcasted_iota(jnp.int32, (2 * count, count), 1)
    allowed = (at_k <= at_q) & (at_k < live)
    column = lanes(count)
    totals = jnp.zeros((count, 128), F32)
    for pair in range(width // 128):
        cut = slice(pair * 128, pair * 128 + 128)
        mixed, log_total = pair_forward(
            stack_pair(q_o[:, cut]), k_o[:, cut], v_o[:, cut],
            lambda scores: jnp.where(allowed, scores, -1e30),
        )
        mix_o[:, cut] = unstack_pair(mixed).astype(BF16)
        totals = jnp.where(column == 2 * pair, log_total[:count], totals)
        totals = jnp.where(column == 2 * pair + 1, log_total[count:], totals)
    lse_o[...] = totals.T
    summed = rows.astype(F32) + nn(mix_o[...], whole(wo))
    sum_o[...] = summed
    normal, _ = norm_parts(summed)
    first = normal * vecs[0:1] + vecs[1:2]
    first_o[...] = first
    low = first.astype(BF16)
    low_o[...] = low
    cq_o[...] = nn(low, whole(wcq)).astype(BF16)


def self_forward(length, tokens, stack, at, vecs):
    count, width = tokens.shape
    low = shape(tokens.shape, BF16)
    wide = shape(tokens.shape, F32)
    spec = full(tokens.shape)
    return call(
        self_body, "self_forward",
        [low, low, low, low, wide, wide, low, low, shape((128, count), F32)], (1,),
        [spec] + [weight(k) for k in at] + [full(vecs.shape)],
        [spec] * 8 + [full((128, count))], prefetch=1,
        flops=10 * count * width * width, moved=16 * MIB,
    )(length, tokens, stack, stack, stack, stack, stack, vecs)


def cross_body(length, q, k, v, mix_o, lse_o):
    count = q.shape[0]
    slots = k.shape[0]
    live = length[0]
    q2 = stack_pair(q[...])
    keys = k[...]
    values = v[...]
    half = slots // 2
    tile = 128
    column = lax.broadcasted_iota(jnp.int32, (tile, slots - half), 1) + half

    def mask(scores):
        upper = jnp.where(column < live, scores[:, half:], -1e30)
        return jnp.concatenate([scores[:, :half], upper], axis=1)

    mixes, logs = [], []
    for at in range(0, 2 * count, tile):
        mixed, log_total = pair_forward(q2[at : at + tile], keys, values, mask)
        mixes.append(mixed)
        logs.append(log_total)
    mix_o[...] = unstack_pair(jnp.concatenate(mixes, axis=0)).astype(BF16)
    logs = jnp.concatenate(logs, axis=0)
    column = lanes(count)
    totals = jnp.where(column == 0, logs[:count], jnp.where(column == 1, logs[count:], 0.0))
    lse_o[0] = totals.T[:8]


def cross_forward(length, q, k, v):
    count, width = q.shape
    slots = k.shape[0]
    pairs = width // 128
    return call(
        cross_body, "cross_forward",
        [shape(q.shape, BF16), shape((pairs, 8, count), F32)], (pairs,),
        [pl.BlockSpec((count, 128), lambda i, _: (0, i))]
        + [pl.BlockSpec((slots, 128), lambda i, _: (0, i))] * 2,
        [pl.BlockSpec((count, 128), lambda i, _: (0, i)), pl.BlockSpec((1, 8, count), lambda i, _: (i, 0, 0))],
        prefetch=1, flops=16 * count * slots * width, moved=10 * MIB,
    )(length, q, k, v)


def second_body(mixture, wo, first, vecs, sum_o, second_o, low_o):
    summed = first[...] + nn(mixture[...], whole(wo))
    sum_o[...] = summed
    normal, _ = norm_parts(summed)
    second = normal * vecs[2:3] + vecs[3:4]
    second_o[...] = second
    low_o[...] = second.astype(BF16)


def second_norm(mixture, stack, at, first, vecs):
    spec = full(mixture.shape)
    return call(
        second_body, "second_norm",
        [shape(mixture.shape, F32), shape(mixture.shape, F32), shape(mixture.shape, BF16)], (1,),
        [spec, weight(at), spec, full(vecs.shape)], [spec] * 3,
        flops=MIB * 512, moved=6 * MIB,
    )(mixture, stack, first, vecs)


def erf(x):
    return lax.erf(x)


def ffn_body(low, second, inner, outer, cot, vecs, act_o, slope_o, out_o, gts_o, go_o, grads_o, total):
    step = pl.program_id(0)
    pre = nn(low[...], whole(inner))
    half = 0.5 * (1.0 + erf(pre * math.sqrt(0.5)))
    active = (pre * half).astype(BF16)
    act_o[...] = active
    slope_o[...] = half + pre * (jnp.exp(-0.5 * pre * pre) * (1.0 / math.sqrt(2.0 * math.pi)))
    part = nn(active, whole(outer))

    @pl.when(step == 0)
    def _():
        total[...] = second[...] + part

    @pl.when(step > 0)
    def _():
        total[...] += part

    @pl.when(step == pl.num_programs(0) - 1)
    def _():
        summed = total[...]
        normal, _ = norm_parts(summed)
        out_o[...] = (normal * vecs[4:5] + vecs[5:6]).astype(BF16)
        grad, gain, shift = norm_back(summed, vecs[4:5], cot[...].astype(F32))
        gts_o[...] = grad
        go_o[...] = grad.astype(BF16)
        grads_o[...] = jnp.concatenate([gain, shift] + [jnp.zeros_like(gain)] * 6, axis=0)


def ffn_forward(low, second, stack, cot, vecs):
    count, width = low.shape
    spec = full(low.shape)
    wide = pl.BlockSpec((count, 1024), lambda i: (0, i))
    return call(
        ffn_body, "ffn_forward",
        [shape((count, 4096), BF16), shape((count, 4096), F32), shape(low.shape, BF16), shape(low.shape, F32), shape(low.shape, BF16), shape((8, width), F32)],
        (4,),
        [spec, spec, pl.BlockSpec((BLOCKS, 32, 1024), lambda i: (0, 4 + i, 0)), pl.BlockSpec((8, 128, 1024), lambda i: (i, 0, 0)), spec, full(vecs.shape)],
        [wide, wide, spec, spec, spec, full((8, width))],
        scratch=[pltpu.VMEM(low.shape, F32)],
        flops=16 * count * width * width, moved=24 * MIB,
    )(low, second, stack, stack, cot, vecs)


def ffn_back_body(go, gts, slope, inner, outer, summed, wo, vecs, gi_o, gss_o, gci_o, gcm_o, grads_o, total):
    step = pl.program_id(0)
    grad = nt(go[...], whole(outer))
    low = (grad * slope[...]).astype(BF16)
    gi_o[...] = low
    part = nt(low, whole(inner))

    @pl.when(step == 0)
    def _():
        total[...] = gts[...] + part

    @pl.when(step > 0)
    def _():
        total[...] += part

    @pl.when(step == pl.num_programs(0) - 1)
    def _():
        grad, gain, shift = norm_back(summed[...], vecs[2:3], total[...])
        gss_o[...] = grad
        low = grad.astype(BF16)
        gci_o[...] = low
        gcm_o[...] = nt(low, whole(wo)).astype(BF16)
        grads_o[...] = jnp.concatenate([gain, shift] + [jnp.zeros_like(gain)] * 6, axis=0)


def ffn_backward(go, gts, slope, stack, summed, squares, at, vecs):
    count, width = go.shape
    spec = full(go.shape)
    wide = pl.BlockSpec((count, 1024), lambda i: (0, i))
    low = shape(go.shape, BF16)
    return call(
        ffn_back_body, "ffn_backward",
        [shape((count, 4096), BF16), shape(go.shape, F32), low, low, shape((8, width), F32)],
        (4,),
        [spec, spec, wide, pl.BlockSpec((BLOCKS, 32, 1024), lambda i: (0, 4 + i, 0)), pl.BlockSpec((8, 128, 1024), lambda i: (i, 0, 0)), spec, weight(at), full(vecs.shape)],
        [wide, spec, spec, spec, full((8, width))],
        scratch=[pltpu.VMEM(go.shape, F32)],
        flops=18 * count * width * width, moved=26 * MIB,
    )(go, gts, slope, stack, stack, summed, squares, vecs)


def cross_back_body(length, q, k, v, g, mixture, lse, dq_o, dk_o, dv_o):
    live = length[0]
    slots = k.shape[0]
    count = q.shape[0]
    q2 = stack_pair(q[...])
    g2 = stack_pair(g[...])
    totals = jnp.concatenate([lse[0, 0:1], lse[0, 1:2]], axis=1) * LOG2E
    inner = pair_inner(mixture[...], g[...])
    tile = 256
    grad_q = jnp.zeros((128, 2 * count), F32)
    for at in range(0, slots, tile):
        mask = None
        if at + tile > slots // 2:
            row = lax.broadcasted_iota(jnp.int32, (tile, 2 * count), 0) + at

            def mask(probs, row=row):
                return jnp.where(row < live, probs, 0.0)

        cut = slice(at, at + tile)
        dq, dk, dv = pair_tile_back(q2, g2, k[cut], v[cut], totals, inner, mask)
        grad_q = grad_q + dq
        dk_o[cut] = dk.astype(BF16)
        dv_o[cut] = dv.astype(BF16)
    dq_o[...] = join_grad_queries(grad_q)


def cross_backward(length, q, k, v, g, mixture, lse):
    count, width = q.shape
    slots = k.shape[0]
    pairs = width // 128
    small = pl.BlockSpec((count, 128), lambda i, _: (0, i))
    large = pl.BlockSpec((slots, 128), lambda i, _: (0, i))
    return call(
        cross_back_body, "cross_backward",
        [shape(q.shape, BF16), shape(k.shape, BF16), shape(k.shape, BF16)], (pairs,),
        [small, large, large, small, small, pl.BlockSpec((1, 8, count), lambda i, _: (i, 0, 0))],
        [small, large, large], prefetch=1,
        flops=40 * count * slots * width, moved=18 * MIB,
    )(length, q, k, v, g, mixture, lse)


def memory_grad_body(dk, dv, wk, wv, out):
    out[...] = nt(dk[...], whole(wk)) + nt(dv[...], whole(wv))


def memory_gradient(dk, dv, stack, at_k, at_v):
    count, width = dk.shape
    tile = 512
    spec = pl.BlockSpec((tile, width), lambda i: (i, 0))
    return call(
        memory_grad_body, "memory_grad", shape(dk.shape, F32), (count // tile,),
        [spec, spec, weight(at_k), weight(at_v)], spec,
        flops=4 * count * width * width, moved=20 * MIB,
    )(dk, dv, stack, stack)


def self_back_body(length, gss, dcq, wcq, summed, wo, vecs, q, k, v, mixture, lse, gfs_o, gsi_o, gq_o, gk_o, gv_o, grads_o):
    live = length[0]
    count, width = gss.shape
    upstream = gss[...] + nt(dcq[...], whole(wcq))
    grad, gain, shift = norm_back(summed[...], vecs[0:1], upstream)
    gfs_o[...] = grad
    grads_o[...] = jnp.concatenate([gain, shift] + [jnp.zeros_like(gain)] * 6, axis=0)
    low = grad.astype(BF16)
    gsi_o[...] = low
    mix_grad = nt(low, whole(wo)).astype(BF16)
    at_k = lax.broadcasted_iota(jnp.int32, (count, 2 * count), 0)
    at_q = lax.rem(lax.broadcasted_iota(jnp.int32, (count, 2 * count), 1), count)
    allowed = (at_k <= at_q) & (at_k < live)
    for pair in range(width // 128):
        cut = slice(pair * 128, pair * 128 + 128)
        g = mix_grad[:, cut]
        totals = jnp.concatenate([lse[2 * pair : 2 * pair + 1], lse[2 * pair + 1 : 2 * pair + 2]], axis=1) * LOG2E
        scores_back = pair_tile_back(
            stack_pair(q[:, cut]), stack_pair(g), k[:, cut], v[:, cut], totals,
            pair_inner(mixture[:, cut], g),
            lambda probs: jnp.where(allowed, probs, 0.0),
        )
        dq, dk, dv = scores_back
        gq_o[:, cut] = join_grad_queries(dq)
        gk_o[:, cut] = dk.astype(BF16)
        gv_o[:, cut] = dv.astype(BF16)


def self_backward(length, gss, dcq, stack, at_cq, at_o, summed, vecs, q, k, v, mixture, lse):
    count, width = q.shape
    spec = full(q.shape)
    low = shape(q.shape, BF16)
    return call(
        self_back_body, "self_backward",
        [shape(q.shape, F32), low, low, low, low, shape((8, width), F32)], (1,),
        [spec, spec, weight(at_cq), spec, weight(at_o), full(vecs.shape), spec, spec, spec, spec, full(lse.shape)],
        [spec] * 5 + [full((8, width))], prefetch=1,
        flops=8 * count * width * width, moved=12 * MIB,
    )(length, gss, dcq, stack, summed, stack, vecs, q, k, v, mixture, lse)


def tokens_grad_body(gfs, gq, gk, gv, wq, wk, wv, out):
    out[...] = gfs[...] + nt(gq[...], whole(wq)) + nt(gk[...], whole(wk)) + nt(gv[...], whole(wv))


def tokens_gradient(gfs, gq, gk, gv, stack, at):
    spec = full(gfs.shape)
    return call(
        tokens_grad_body, "tokens_grad", shape(gfs.shape, F32), (1,),
        [spec] * 4 + [weight(k) for k in at], spec,
        flops=6 * MIB * 256, moved=10 * MIB,
    )(gfs, gq, gk, gv, stack, stack, stack)


def place(keep, send, at, size, pieces, me):
    low = lax.rem(me, 8)
    for j in range(8):
        rows = pieces(lax.bitwise_xor(low, j))
        target = send if j % 2 else keep
        target[j // 2, at : at + size, :] = rows.astype(BF16)


def outer_body(me, act, go, keep, send, held):
    held[...] = tn(act[...], go[...])
    place(keep, send, 0, 128, lambda d: held[pl.ds(pl.multiple_of(d * 128, 128), 128), :], me[0])


def inner_body(me, low, gi, keep, send, held):
    for part in range(4):
        held[...] = tn(low[...], gi[:, part * 1024 : part * 1024 + 1024])
        place(keep, send, part * 32, 32, lambda d: held[pl.ds(pl.multiple_of(d * 32, 32), 32), :], me[0])


def group_of(step, me):
    return lax.bitwise_xor(step, lax.div(me[0], 8))


def payload(rows, width):
    out = [shape((16, rows, width), BF16)] * 2
    spec = [pl.BlockSpec((4, rows, width), lambda i, _: (i, 0, 0))] * 2
    return out, spec


def outer_weights(me, act, go):
    count, width = go.shape
    out, spec = payload(128, width)
    return call(
        outer_body, "outer_weights", out, (4,),
        [pl.BlockSpec((count, 1024), lambda i, me: (0, group_of(i, me))), full(go.shape)],
        spec, [pltpu.VMEM((1024, width), F32)], 1,
        flops=8 * count * width * width, moved=11 * MIB,
    )(me, act, go)


def inner_weights(me, low, gi):
    count, width = low.shape
    out, spec = payload(128, width)
    return call(
        inner_body, "inner_weights", out, (4,),
        [pl.BlockSpec((count, 256), lambda i, me: (0, group_of(i, me))), full(gi.shape)],
        spec, [pltpu.VMEM((256, width), F32)], 1,
        flops=8 * count * width * width, moved=11 * MIB,
    )(me, low, gi)


def square_body(me, *refs):
    count = (len(refs) - 3) // 2
    keep, send, held = refs[-3:]
    for at in range(count):
        held[...] = tn(refs[2 * at][...], refs[2 * at + 1][...])
        place(keep, send, at * 32, 32, lambda d: held[pl.ds(pl.multiple_of(d * 32, 32), 32), :], me[0])


def square_vec_body(me, *refs):
    vecs = refs[-4]
    square_body(me, *refs[:-4], *refs[-3:])
    keep, send = refs[-3:-1]
    rows = vecs[...]
    step = group_of(pl.program_id(0), me)
    width = rows.shape[1]

    def pieces(d):
        return pltpu.roll(rows, lax.rem(width - (step * 8 + d) * 32, width), 1)

    place(keep, send, 128, 16, pieces, me[0])


def square_weights(me, pairs, name, vecs=None):
    width = pairs[0][0].shape[1]
    out, spec = payload(128 if vecs is None else 144, width)
    ins, operands, flops = [], [], 0
    for rows, grads in pairs:
        ins.append(pl.BlockSpec((rows.shape[0], 256), lambda i, me: (0, group_of(i, me))))
        ins.append(full(grads.shape))
        operands += [rows, grads]
        flops += 2 * rows.shape[0] * width * width
    if vecs is not None:
        ins.append(full(vecs.shape))
        operands.append(vecs)
    return call(
        square_body if vecs is None else square_vec_body, name, out, (4,), ins, spec,
        [pltpu.VMEM((256, width), F32)], 1, flops=flops, moved=20 * MIB,
    )(me, *operands)


def swap(rows, distance):
    return lax.ppermute(rows, "dp", [(i, i ^ distance) for i in range(BLOCKS)])


def scatter_sum(keep, send):
    rows, width = keep.shape[1:]
    cut = (rows // 32) * 16
    came = swap(send, 1)
    dims = (2, 2, 2, 2, rows, width)
    keep, came = keep.reshape(dims), came.reshape(dims)

    def start(index, part):
        return keep[index][..., part, :].astype(F32) + came[index][..., part, :].astype(F32)

    a, b = slice(0, cut), slice(cut, rows)
    every = slice(None)
    a_came = swap(start((every, every, every, 1), a).astype(BF16), 2)
    b_came = swap(start((every, every, 1), b).astype(BF16), 4)

    def a_second(at):
        return start((every, every, at, 0), a) + a_came[:, :, at].astype(F32)

    def b_second(at):
        return start((every, every, 0, at), b) + b_came[:, :, at].astype(F32)

    a_more = swap(a_second(1).astype(BF16), 4)
    b_more = swap(b_second(1).astype(BF16), 2)

    def third(at):
        return jnp.concatenate(
            [a_second(0)[at] + a_more[at].astype(F32), b_second(0)[at] + b_more[at].astype(F32)], axis=-2
        )

    far = swap(third(1).astype(BF16), 16)

    def fourth(at):
        return third(0)[at] + far[at].astype(F32)

    near = swap(fourth(1).astype(BF16), 8)
    return fourth(0) + near.astype(F32)


def absolute(keep, send):
    return jnp.stack([keep, send], axis=1).reshape((BLOCKS,) + keep.shape[1:])


def pack_vectors(vectors, devices):
    own = vectors[0].shape[0]
    rows = jnp.stack(vectors)
    return jnp.pad(rows, ((0, 16 - len(vectors)), (0, 1024 - own)))


def gather(rows):
    return lax.all_gather(rows, "dp", axis=0, tiled=True)


def on_device(
    devices, tokens, memory, target_lengths, memory_lengths, cotangent,
    self_query, self_key, self_value, self_output, first_gain, first_shift,
    cross_query, cross_key, cross_value, cross_output, second_gain, second_shift,
    inner_weight, outer_weight, third_gain, third_shift,
):
    width = tokens.shape[1]
    hidden = inner_weight.shape[1]
    direct = devices == BLOCKS
    squares = [cross_key, cross_value, self_query, self_key, self_value, self_output, cross_query, cross_output]
    vectors = [first_gain, first_shift, second_gain, second_shift, third_gain, third_shift]
    if direct:
        me = lax.axis_index("dp").astype(jnp.int32).reshape(1)
        pack = jnp.concatenate(squares + [pack_vectors(vectors, devices)], axis=0)
        stack = gather(pack).reshape(BLOCKS, -1, width)
        vecs = stack[:, 256:264, :32].transpose(1, 0, 2).reshape(8, width).astype(F32)
        parts = [outer_weight] + [inner_weight[:, i : i + width] for i in range(0, hidden, width)]
        pack = jnp.concatenate(parts, axis=0)
        pack, _ = lax.optimization_barrier((pack, stack[0, :1]))
        wide = gather(pack).reshape(BLOCKS, -1, width)
    else:
        me = jnp.zeros((1,), jnp.int32)
        stack = jnp.concatenate([gather(w).reshape(BLOCKS, 32, width) for w in squares], axis=1)
        vecs = jnp.pad(jnp.stack([gather(v) for v in vectors]), ((0, 2), (0, 0))).astype(F32)
        inner_full = gather(inner_weight)
        parts = [gather(outer_weight).reshape(BLOCKS, 128, width)]
        parts += [inner_full[:, i : i + width].reshape(BLOCKS, 32, width) for i in range(0, hidden, width)]
        wide = jnp.concatenate(parts, axis=1)

    keys, values = kv_project(memory, stack, 0, 1)
    q, k, v, mixture, first_sum, first_out, first_low, cross_q, lse = self_forward(
        target_lengths, tokens, stack, (2, 3, 4, 5, 6), vecs
    )
    cross_mixture, cross_lse = cross_forward(memory_lengths, cross_q, keys, values)
    second_sum, second, second_low = second_norm(cross_mixture, stack, 7, first_out, vecs)
    act, slope, output_rows, gts, go, third_grads = ffn_forward(second_low, second, wide, cotangent, vecs)
    outer_pay = outer_weights(me, act, go)
    gi, gss, gci, gcm, second_grads = ffn_backward(go, gts, slope, wide, second_sum, stack, 7, vecs)
    inner_pay = inner_weights(me, second_low, gi)
    dq, dk, dv = cross_backward(memory_lengths, cross_q, keys, values, gcm, cross_mixture, cross_lse)
    cross_pay = square_weights(
        me, [(first_low, dq), (memory, dk), (memory, dv), (cross_mixture, gci)], "cross_weights"
    )
    gfs, gsi, gq, gk, gv, first_grads = self_backward(
        target_lengths, gss, dq, stack, 6, 5, first_sum, vecs, q, k, v, mixture, lse
    )
    grads = jnp.concatenate([first_grads[:2], second_grads[:2], third_grads[:2], jnp.zeros((10, width), F32)])
    self_pay = square_weights(me, [(tokens, gq), (tokens, gk), (tokens, gv), (mixture, gsi)], "self_weights", grads)
    memory_grad = memory_gradient(dk, dv, stack, 0, 1)
    tokens_grad = tokens_gradient(gfs, gq, gk, gv, stack, (2, 3, 4))

    if direct:
        outer_own = scatter_sum(*outer_pay)
        inner_own = scatter_sum(*inner_pay)
        cross_own = scatter_sum(*cross_pay)
        self_own = scatter_sum(*self_pay)
        inner_own = jnp.concatenate([inner_own[i : i + 32] for i in range(0, 128, 32)], axis=1)
        cross_own = [cross_own[i : i + 32] for i in range(0, 128, 32)]
        vec_own = [self_own[128 + i, :32] for i in range(6)]
        self_own = [self_own[i : i + 32] for i in range(0, 128, 32)]
    else:
        def owned(rows):
            return lax.psum_scatter(rows.astype(F32), "dp", scatter_dimension=0, tiled=True)

        outer_own = owned(absolute(*outer_pay).reshape(-1, width))
        inner_rows = absolute(*inner_pay)
        inner_rows = jnp.concatenate([inner_rows[:, i : i + 32].reshape(-1, width) for i in range(0, 128, 32)], axis=1)
        inner_own = owned(inner_rows)
        cross_rows, self_rows = absolute(*cross_pay), absolute(*self_pay)
        cross_own = [owned(cross_rows[:, i : i + 32].reshape(-1, width)) for i in range(0, 128, 32)]
        self_own = [owned(self_rows[:, i : i + 32].reshape(-1, width)) for i in range(0, 128, 32)]
        vec_own = [owned(grads[i]) for i in range(6)]

    return (
        output_rows, tokens_grad, memory_grad,
        *self_own, vec_own[0], vec_own[1],
        *cross_own, vec_own[2], vec_own[3],
        inner_own, outer_own, vec_own[4], vec_own[5],
    )


def solution(mesh):
    rows, line = P("dp", None), P("dp")
    block = [rows] * 4 + [line] * 2
    placed = (rows, rows, line, line, rows, *block, *block, rows, rows, line, line)
    return jax.shard_map(
        functools.partial(on_device, mesh.shape["dp"]),
        mesh=mesh,
        in_specs=placed,
        out_specs=(rows, rows, rows, *block, *block, rows, rows, line, line),
        check_vma=False,
    )
```

time: 2240 us -> 653 us (0.29)
  waiting for transfers between devices: 1690 us -> 343 us
  matrix products: 252 us -> 0 us
  Pallas kernels: 0 us -> 172 us
  local copies, waits for them, and re-layouts: 143 us -> 52.3 us
  blocking collectives: 81.9 us -> 0 us
  starting transfers between devices: 1.01 us -> 36.7 us
  other arithmetic: 47.4 us -> 22.7 us
    reduce_scatter x10 -> x0, waiting for transfers between devices: 1210 us -> none  [the longest x1 214 us: on_device(): lax.psum_scatter(flatten_rows(grad_inner_weight), 'dp', scatter_dimension...]
    all_gather x10 -> x2, waiting for transfers between devices: 474 us -> 183 us  [gather(): return lax.all_gather(rows, 'dp', axis=0, tiled=True)]
    dot_general x42 -> x0, matrix products: 252 us -> none  [the longest x10 56.1 us: matmul(): return jnp.dot(operand, factor, preferred_element_type=jnp.float32)]
    pallas_call x0 -> x14, Pallas kernels: none -> 172 us  [the longest x1 26.7 us: cross_backward(): call(cross_back_body, 'cross_backward', [shape(q.shape, BF16), shape(k.sh...]
    ppermute x0 -> x28, waiting for transfers between devices: none -> 160 us  [swap(): return lax.ppermute(rows, 'dp', [(i, i ^ distance) for i in range(BLOCKS)])]
    reshape x20 -> x0, local copies, waits for them, and re-layouts: 92.1 us -> none  [the longest x10 75.5 us: flatten_rows(): return matrix.reshape(-1, 128)]
    unnamed x2 -> x0, blocking collectives: 81.9 us -> none
    ppermute x0 -> x28, starting transfers between devices: none -> 36.6 us  [swap(): return lax.ppermute(rows, 'dp', [(i, i ^ distance) for i in range(BLOCKS)])]
  transfers between devices with their start and end apart: 20 -> 30, of which waited for: 18 -> 17; matrix products, arithmetic and copies ran while one was open for 14% -> 10% of each run, Pallas kernels for 0% -> 16%
where the time goes in v1:
time: 653 us; the launch traced here: 643 us
  waiting for transfers between devices  343 us (53%)
  Pallas kernels  172 us (26%)
  local copies, waits for them, and re-layouts  52.3 us (8%)
  starting transfers between devices  36.7 us (6%)
  other arithmetic  22.7 us (3%)
  between operations  16.1 us (2%)
    all_gather x2, waiting for transfers between devices, gather(): return lax.all_gather(rows, 'dp', axis=0, tiled=True)  183 us
    ppermute x28, waiting for transfers between devices, swap(): return lax.ppermute(rows, 'dp', [(i, i ^ distance) for i in range(BLOCKS)])  160 us
    ppermute x28, starting transfers between devices, swap(): return lax.ppermute(rows, 'dp', [(i, i ^ distance) for i in range(BLOCKS)])  36.6 us
    squeeze x12, local copies, waits for them, and re-layouts, start(): came[index][..., part, :].astype(F32)  27 us
    pallas_call x1, Pallas kernels, cross_backward(): call(cross_back_body, 'cross_backward', [shape(q.shape, BF16), shape(k.sh...  26.7 us
    pallas_call x2, Pallas kernels, square_weights(): call(square_body if vecs is None else square_vec_body, name, out, (4,), i...  25 us
    pallas_call x1, Pallas kernels, cross_forward(): call(cross_body, 'cross_forward', [shape(q.shape, BF16), shape((pairs, 8,...  20 us
    pallas_call x1, Pallas kernels, ffn_backward(): call(ffn_back_body, 'ffn_backward', [shape((count, 4096), BF16), shape(go...  14.2 us
  transfers between devices with their start and end apart: 30, of which 17 were waited for; matrix products, arithmetic and copies ran while one was open for 10% of the time, Pallas kernels for 16%

profile of v1, /device:TPU:14, one launch (start us, length us, event | category | flops | bytes accessed | tf_op | source)
XLA Modules:
  0.0 643.1 jit_solution(1605599025121956805)
XLA Ops:
  18.8 115.7 %all-gather.3.cloned.1.call-done = bf16[8704,1024]{1,0:T(8,128)(2,1)} async-done(((bf16[272,1024]{1,0:T(8,128)(2,1)}), bf16[8704,1024]{1,0:T(8,128)(2,1)}) %all-gather.3.cloned.1.call-update) | async-done | bytes 17825808 | tf_op jit(solution)/shard_map/all_gather | solution.py:609
  136.2 10.1 %self_forward.1 = (bf16[256,1024]{1,0:T(8,128)(2,1)}, bf16[256,1024]{1,0:T(8,128)(2,1)}, bf16[256,1024]{1,0:T(8,128)(2,1)}, bf16[256,1024]{1,0:T(8,128)(2,1)}, f...) custom-call(s32[1]{0:T(128)S(6)} %copy.189.length, ...), custom_call_target="tpu_custom_call" | custom-call | flops 2684354560 | bytes 16777216 | tf_op jit(solution)/shard_map/self_forward/pallas_call | solution.py:198
  146.3 13.4 %cross_kv.1 = (bf16[2048,1024]{1,0:T(8,128)(2,1)}, bf16[2048,1024]{1,0:T(8,128)(2,1)}) custom-call(bf16[2048,1024]{1,0:T(8,128)(2,1)} %refs_4_.3, bf16[32,272,1024]{2,1,0:T(8,128)(2,1)} %bitcast.301, bf16[32,272,1024]{2,1,0:T(8,128)(2,1)} %bitcast.302), custom_call_target="tpu_custom_call" | custom-call | flops 8589934592 | bytes 16777216 | tf_op jit(solution)/shard_map/cross_kv/pallas_call | solution.py:154
  159.8 20.0 %cross_forward.1 = (bf16[256,1024]{1,0:T(8,128)(2,1)}, f32[8,8,256]{2,1,0:T(8,128)}) custom-call(s32[1]{0:T(128)S(6)} %copy.190.length, bf16[256,1024]{1,0:T(8,128)(2,1)} %get-tuple-element.63.q, bf16[2048,1024]{1,0:T(8,128)(2,1)} %get-tuple-element.64.k, bf16[2048,1024]{1,0:T(8,128)(2,1)} %get-tuple-element.65.v), custom_call_target="tpu_custom_call" | custom-call | flops 8589934592 | bytes 10485760 | tf_op jit(solution)/shard_map/cross_forward/pallas_call | solution.py:238
  179.7 4.2 second_norm.1
  184.0 67.2 %all-gather.5.cloned.1.call-done = bf16[8192,1024]{1,0:T(8,128)(2,1)} async-done(((bf16[256,1024]{1,0:T(8,128)(2,1)}), bf16[8192,1024]{1,0:T(8,128)(2,1)}) %all-gather.5.cloned.1.call-update) | async-done | bytes 16777232 | tf_op jit(solution)/shard_map/all_gather | solution.py:609
  251.2 13.7 %ffn_forward.1 = (bf16[256,4096]{1,0:T(8,128)(2,1)}, f32[256,4096]{1,0:T(8,128)}, bf16[256,1024]{1,0:T(8,128)(2,1)}, f32[256,1024]{1,0:T(8,128)}, bf16[256,1024]{1,0:T(8,128)(2,1)}, /*index=5*/f32[8,1024]{1,0:T(8,128)}) custom-call(bf16[256,1024]{1,0:T(8,128)(2,1)} %get-tuple-element.68.low, f32[256,1024]{1,0:T(8,128)} %get-tuple-element.69.second, ...), custom_call_target="tpu_custom_call" | custom-call | flops 4294967296 | bytes 25165824 | tf_op jit(solution)/shard_map/ffn_forward/pallas_call | solution.py:303
  264.9 14.2 %ffn_backward.1 = (bf16[256,4096]{1,0:T(8,128)(2,1)}, f32[256,1024]{1,0:T(8,128)}, bf16[256,1024]{1,0:T(8,128)(2,1)}, bf16[256,1024]{1,0:T(8,128)(2,1)}, f32[8,1024]{1,0:T(8,128)}) custom-call(bf16[256,1024]{1,0:T(8,128)(2,1)} %get-tuple-element.71.go, f32[256,1024]{1,0:T(8,128)} %get-tuple-element.72.gts, f32[256,4096]{1,0:T(8,128)} %get-tuple-element.73.slope, ...), custom_call_target="tpu_custom_call" | custom-call | flops 4831838208 | bytes 27262976 | tf_op jit(solution)/shard_map/ffn_backward/pallas_call | solution.py:344
  279.1 26.7 %cross_backward.1 = (bf16[256,1024]{1,0:T(8,128)(2,1)}, bf16[2048,1024]{1,0:T(8,128)(2,1)}, bf16[2048,1024]{1,0:T(8,128)(2,1)}) custom-call(s32[1]{0:T(128)S(6)} %copy.190.length, bf16[256,1024]{1,0:T(8,128)(2,1)} %get-tuple-element.63.q, bf16[2048,1024]{1,0:T(8,128)(2,1)} %get-tuple-element.64.k, bf16[2048,1024]{1,0:T(8,128)(2,1)} %get-tuple-element.65.v, ...), custom_call_target="tpu_custom_call" | custom-call | flops 21474836480 | bytes 18874368 | tf_op jit(solution)/shard_map/cross_backward/pallas_call | solution.py:387
  305.8 17.0 %cross_weights.1 = (bf16[16,128,1024]{2,1,0:T(8,128)(2,1)}, bf16[16,128,1024]{2,1,0:T(8,128)(2,1)}) custom-call(s32[1]{0:T(128)} %bitcast.9.me, bf16[256,1024]{1,0:T(8,128)(2,1)} %get-tuple-element.97.refs_0_, bf16[256,1024]{1,0:T(8,128)(2,1)} %get-tuple-element.78.dcq.refs_1_, bf16[2048,1024]{1,0:T(8,128)(2,1)} %refs_4_.3, ...), custom_call_target="tpu_custom_call" | custom-call | flops 9663676416 | bytes 20971520 | tf_op jit(solution)/shard_map/cross_weights/pallas_call | solution.py:550
  324.6 9.9 %self_backward.1 = (f32[256,1024]{1,0:T(8,128)}, bf16[256,1024]{1,0:T(8,128)(2,1)}, bf16[256,1024]{1,0:T(8,128)(2,1)}, bf16[256,1024]{1,0:T(8,128)(2,1)}, bf16[256,1024]{1,0:T(8,128)(2,1)}, /*index=5*/f32[8,1024]{1,0:T(8,128)}) custom-call(s32[1]{0:T(128)S(6)} %copy.189.length, f32[256,1024]{1,0:T(8,128)} %get-tuple-element.75.gss, ...), custom_call_target="tpu_custom_call" | custom-call | flops 2147483648 | bytes 12582912 | tf_op jit(solution)/shard_map/self_backward/pallas_call | solution.py:443
  335.3 7.1 %inner_weights.1 = (bf16[16,128,1024]{2,1,0:T(8,128)(2,1)}, bf16[16,128,1024]{2,1,0:T(8,128)(2,1)}) custom-call(s32[1]{0:T(128)} %bitcast.9.me, bf16[256,1024]{1,0:T(8,128)(2,1)} %get-tuple-element.68.low, bf16[256,4096]{1,0:T(8,128)(2,1)} %get-tuple-element.101.gi), custom_call_target="tpu_custom_call" | custom-call | flops 2147483648 | bytes 11534336 | tf_op jit(solution)/shard_map/inner_weights/pallas_call | solution.py:508
  343.4 8.0 %self_weights.1 = (bf16[16,144,1024]{2,1,0:T(8,128)(2,1)}, bf16[16,144,1024]{2,1,0:T(8,128)(2,1)}) custom-call(s32[1]{0:T(128)} %bitcast.9.me, bf16[256,1024]{1,0:T(8,128)(2,1)} %refs_4_.2, bf16[256,1024]{1,0:T(8,128)(2,1)} %get-tuple-element.86.gq.refs_1_, bf16[256,1024]{1,0:T(8,128)(2,1)} %refs_4_.2, bf16[256,1024]{1,0:T(8,128)(2,1)} %get-tuple-element.87.gk.refs_3_, ...), custom_call_target="tpu_custom_call" | custom-call | flops 2147483648 | bytes 20971520 | tf_op jit(solution)/shard_map/self_weights/pallas_call | solution.py:550
  351.6 7.1 %outer_weights.1 = (bf16[16,128,1024]{2,1,0:T(8,128)(2,1)}, bf16[16,128,1024]{2,1,0:T(8,128)(2,1)}) custom-call(s32[1]{0:T(128)} %bitcast.9.me, bf16[256,4096]{1,0:T(8,128)(2,1)} %get-tuple-element.104.act, bf16[256,1024]{1,0:T(8,128)(2,1)} %get-tuple-element.71.go), custom_call_target="tpu_custom_call" | custom-call | flops 2147483648 | bytes 11534336 | tf_op jit(solution)/shard_map/outer_weights/pallas_call | solution.py:497
  359.0 1.7 slice_bitcast_fusion.19
  360.7 1.6 copy-done.2
  362.4 1.7 slice_bitcast_fusion.13
  365.3 1.8 slice_bitcast_fusion.7
  367.1 6.6 %tokens_grad.1 = f32[256,1024]{1,0:T(8,128)} custom-call(f32[256,1024]{1,0:T(8,128)} %get-tuple-element.85.gfs, bf16[256,1024]{1,0:T(8,128)(2,1)} %get-tuple-element.86.gq.refs_1_, bf16[256,1024]{1,0:T(8,128)(2,1)} %get-tuple-element.87.gk.refs_3_, bf16[256,1024]{1,0:T(8,128)(2,1)} %get-tuple-element.88.gv.refs_5_, bf16[32,272,1024]{2,1,0:T(8,128)(2,1)} %bitcast.307, ...), custom_call_target="tpu_custom_call" | custom-call | flops 1610612736 | bytes 10485760 | tf_op jit(solution)/shard_map/tokens_grad/pallas_call | solution.py:458
  373.6 1.8 slice_bitcast_fusion.1
  375.4 13.9 %memory_grad.1 = f32[2048,1024]{1,0:T(8,128)} custom-call(bf16[2048,1024]{1,0:T(8,128)(2,1)} %get-tuple-element.89.dk.refs_3_, bf16[2048,1024]{1,0:T(8,128)(2,1)} %get-tuple-element.90.dv.refs_5_, bf16[32,272,1024]{2,1,0:T(8,128)(2,1)} %bitcast.310, bf16[32,272,1024]{2,1,0:T(8,128)(2,1)} %bitcast.311), custom_call_target="tpu_custom_call" | custom-call | flops 8589934592 | bytes 20971520 | tf_op jit(solution)/shard_map/memory_grad/pallas_call | solution.py:404
  389.4 2.9 copy_bitcast_fusion.12
  394.9 2.3 copy_bitcast_fusion.14
  397.2 1.4 add_convert_fusion.6
  399.4 2.1 copy_bitcast_fusion.8
  401.5 1.4 add_convert_fusion.3
  402.9 1.5 collective-permute-start.17
  404.4 2.3 copy_bitcast_fusion.10
  408.7 2.1 copy_bitcast_fusion.4
  411.2 2.1 copy_bitcast_fusion.6
  414.7 2.2 slice_bitcast_fusion.18
  416.9 2.2 slice_bitcast_fusion.12
  419.1 2.2 slice_bitcast_fusion.6
  422.6 2.2 copy_bitcast_fusion
  425.3 2.2 copy_bitcast_fusion.2
  427.5 2.4 slice_bitcast_fusion
  432.6 2.2 convert_add_fusion.11
  434.9 7.4 %collective-permute-done.17 = bf16[2,2,2,64,1024]{4,3,1,0,2:T(8,128)(2,1)S(1)} collective-permute-done((bf16[2,2,2,64,1024]{4,3,1,0,2:T(8,128)(2,1)}, bf16[2,2,2,64,1024]{4,3,1,0,2:T(8,128)(2,1)S(1)}, u32[]{:S(2)}, u32[]{:S(2)}) %collective-permute-start.17) | collective-permute-done | bytes 1048608 | tf_op jit(solution)/shard_map/ppermute | solution.py:557
  443.6 3.8 collective-permute-done.15
  448.1 1.7 convert_add_fusion.7
  449.8 15.1 %collective-permute-done.24 = bf16[2,2,2,64,1024]{4,3,1,0,2:T(8,128)(2,1)} collective-permute-done((bf16[2,2,2,64,1024]{4,3,1,0,2:T(8,128)(2,1)S(1)}, bf16[2,2,2,64,1024]{4,3,1,0,2:T(8,128)(2,1)}, u32[]{:S(2)}, u32[]{:S(2)}) %collective-permute-start.24) | collective-permute-done | bytes 1048608 | tf_op jit(solution)/shard_map/ppermute | solution.py:557
  464.9 1.5 collective-permute-start.11
  466.4 3.4 collective-permute-done.22
  470.6 2.6 convert_add_fusion.3
  473.2 19.0 %collective-permute-done.1 = bf16[2,2,2,64,1024]{4,3,1,0,2:T(8,128)(2,1)S(1)} collective-permute-done((bf16[2,2,2,64,1024]{4,3,1,0,2:T(8,128)(2,1)S(1)}, bf16[2,2,2,64,1024]{4,3,1,0,2:T(8,128)(2,1)S(1)}, u32[]{:S(2)}, u32[]{:S(2)}) %collective-permute-start.1) | collective-permute-done | bytes 1048608 | tf_op jit(solution)/shard_map/ppermute | solution.py:557
  493.0 1.6 fusion.7
  494.7 9.4 %collective-permute-done.9 = bf16[2,2,64,1024]{3,2,1,0:T(8,128)(2,1)S(1)} collective-permute-done((bf16[2,2,64,1024]{3,2,1,0:T(8,128)(2,1)}, bf16[2,2,64,1024]{3,2,1,0:T(8,128)(2,1)S(1)}, u32[]{:S(2)}, u32[]{:S(2)}) %collective-permute-start.9) | collective-permute-done | bytes 524320 | tf_op jit(solution)/shard_map/ppermute | solution.py:557
  506.5 8.8 %collective-permute-done.16 = bf16[2,2,64,1024]{3,2,1,0:T(8,128)(2,1)S(1)} collective-permute-done((bf16[2,2,64,1024]{3,2,1,0:T(8,128)(2,1)S(1)}, bf16[2,2,64,1024]{3,2,1,0:T(8,128)(2,1)S(1)}, u32[]{:S(2)}, u32[]{:S(2)}) %collective-permute-start.16) | collective-permute-done | bytes 524320 | tf_op jit(solution)/shard_map/ppermute | solution.py:557
  516.8 1.8 collective-permute-start.12
  518.8 7.7 %collective-permute-done.23 = bf16[2,2,64,1024]{3,2,1,0:T(8,128)(2,1)S(1)} collective-permute-done((bf16[2,2,64,1024]{3,2,1,0:T(8,128)(2,1)S(1)}, bf16[2,2,64,1024]{3,2,1,0:T(8,128)(2,1)S(1)}, u32[]{:S(2)}, u32[]{:S(2)}) %collective-permute-start.23) | collective-permute-done | bytes 524320 | tf_op jit(solution)/shard_map/ppermute | solution.py:557
  526.6 1.8 collective-permute-start.19
  530.8 1.5 collective-permute-start.4
  532.3 30.9 %collective-permute-done.12 = bf16[2,128,1024]{2,1,0:T(8,128)(2,1)S(1)} collective-permute-done((bf16[2,128,1024]{2,1,0:T(8,128)(2,1)S(1)}, bf16[2,128,1024]{2,1,0:T(8,128)(2,1)S(1)}, u32[]{:S(2)}, u32[]{:S(2)}) %collective-permute-start.12) | collective-permute-done | bytes 524320 | tf_op jit(solution)/shard_map/ppermute | solution.py:557
  563.3 2.2 collective-permute-start.13
  565.5 9.1 %collective-permute-done.19 = bf16[2,128,1024]{2,1,0:T(8,128)(2,1)S(1)} collective-permute-done((bf16[2,128,1024]{2,1,0:T(8,128)(2,1)S(1)}, bf16[2,128,1024]{2,1,0:T(8,128)(2,1)S(1)}, u32[]{:S(2)}, u32[]{:S(2)}) %collective-permute-start.19) | collective-permute-done | bytes 524320 | tf_op jit(solution)/shard_map/ppermute | solution.py:557
  574.6 2.2 collective-permute-start.20
  576.8 7.9 %collective-permute-done.26 = bf16[2,128,1024]{2,1,0:T(8,128)(2,1)S(1)} collective-permute-done((bf16[2,128,1024]{2,1,0:T(8,128)(2,1)S(1)}, bf16[2,128,1024]{2,1,0:T(8,128)(2,1)S(1)}, u32[]{:S(2)}, u32[]{:S(2)}) %collective-permute-start.26) | collective-permute-done | bytes 524320 | tf_op jit(solution)/shard_map/ppermute | solution.py:557
  584.8 3.2 collective-permute-start.27
  588.1 2.8 collective-permute-done.13
  591.0 5.5 collective-permute-done.20
  596.9 2.9 collective-permute-start.5
  600.6 23.9 %collective-permute-done.5 = bf16[2,144,1024]{2,1,0:T(8,128)(2,1)S(1)} collective-permute-done((bf16[2,144,1024]{2,1,0:T(8,128)(2,1)S(1)}, bf16[2,144,1024]{2,1,0:T(8,128)(2,1)S(1)}, u32[]{:S(2)}, u32[]{:S(2)}) %collective-permute-start.5) | collective-permute-done | bytes 589856 | tf_op jit(solution)/shard_map/ppermute | solution.py:557
  624.6 2.9 collective-permute-start.6
  629.1 5.5 collective-permute-done.6
  (131 shorter events, 43.7 us)
Async XLA Ops:
  7.2 9.5 %copy-start.17 = (bf16[32,4096]{1,0:T(8,128)(2,1)S(1)}, bf16[32,4096]{1,0:T(8,128)(2,1)}, u32[]{:S(2)}) copy-start(bf16[32,4096]{1,0:T(8,128)(2,1)} %param.38) | copy-start | bytes 786436
  7.2 127.4 %all-gather.3.cloned.1.call-start = ((), (), s32[]{:S(2)}) async-start(), calls=%async_computation | async-start | bytes 18382848 | tf_op jit(solution)/shard_map/all_gather | solution.py:609
  14.8 0.8 copy-start.16
  15.6 235.6 %all-gather.5.cloned.1.call-start = ((), (), s32[]{:S(2)}) async-start(), calls=%async_computation.1 | async-start | bytes 17301504 | tf_op jit(solution)/shard_map/all_gather | solution.py:609
  16.7 0.8 copy-start.14
  322.8 66.6 %collective-permute-start.7 = (bf16[16,128,1024]{2,1,0:T(8,128)(2,1)}, bf16[16,128,1024]{2,1,0:T(8,128)(2,1)}, u32[]{:S(2)}, u32[]{:S(2)}) collective-permute-start(bf16[16,128,1024]{2,1,0:T(8,128)(2,1)} %get-tuple-element.100), channel_id=1, source_target_pairs={{0,1},{1,0},{2,3},{3,2},{4,5},{5,4},{6,7},{7,6},{8,9},{9,8},{10,11... | collective-permute-start | bytes 12582920 | tf_op jit(solution)/shard_map/ppermute | solution.py:557
  342.4 57.0 %collective-permute-start.14 = (bf16[16,128,1024]{2,1,0:T(8,128)(2,1)}, bf16[16,128,1024]{2,1,0:T(8,128)(2,1)}, u32[]{:S(2)}, u32[]{:S(2)}) collective-permute-start(bf16[16,128,1024]{2,1,0:T(8,128)(2,1)} %get-tuple-element.103), channel_id=1, source_target_pairs={{0,1},{1,0},{2,3},{3,2},{4,5},{5,4},{6,7},{7,6},{8,9},{9,8},{10,11... | collective-permute-start | bytes 12582920 | tf_op jit(solution)/shard_map/ppermute | solution.py:557
  351.4 69.8 %collective-permute-start = (bf16[16,144,1024]{2,1,0:T(8,128)(2,1)}, bf16[16,144,1024]{2,1,0:T(8,128)(2,1)}, u32[]{:S(2)}, u32[]{:S(2)}) collective-permute-start(bf16[16,144,1024]{2,1,0:T(8,128)(2,1)} %get-tuple-element.96), channel_id=1, source_target_pairs={{0,1},{1,0},{2,3},{3,2},{4,5},{5,4},{6,7},{7,6},{8,9},{9,8},{10,11... | collective-permute-start | bytes 14155784 | tf_op jit(solution)/shard_map/ppermute | solution.py:557
  351.6 7.4 %copy-start = (bf16[16,128,1024]{2,1,0:T(8,128)(2,1)S(1)}, bf16[16,128,1024]{2,1,0:T(8,128)(2,1)}, u32[]{:S(2)}) copy-start(bf16[16,128,1024]{2,1,0:T(8,128)(2,1)} %get-tuple-element.99) | copy-start | bytes 12582916
  358.8 49.3 %collective-permute-start.21 = (bf16[16,128,1024]{2,1,0:T(8,128)(2,1)}, bf16[16,128,1024]{2,1,0:T(8,128)(2,1)}, u32[]{:S(2)}, u32[]{:S(2)}) collective-permute-start(bf16[16,128,1024]{2,1,0:T(8,128)(2,1)} %get-tuple-element.106), channel_id=1, source_target_pairs={{0,1},{1,0},{2,3},{3,2},{4,5},{5,4},{6,7},{7,6},{8,9},{9,8},{10,11... | collective-permute-start | bytes 12582920 | tf_op jit(solution)/shard_map/ppermute | solution.py:557
  359.0 3.3 copy-start.2
  362.4 2.9 copy-start.4
  367.1 6.6 %slice-start = ((s8[4718592]{0:T(1024)(128)(4,1)}), s8[4194304]{0:T(1024)(128)(4,1)S(1)}, s32[]{:S(2)}) async-start(s8[4718592]{0:T(1024)(128)(4,1)} %bitcast.316), calls=%async_computation.2 | async-start | bytes 8388608
  367.1 6.6 %slice-start.1 = ((s8[4718592]{0:T(1024)(128)(4,1)}), s8[524288]{0:T(1024)(128)(4,1)S(1)}, s32[]{:S(2)}) async-start(s8[4718592]{0:T(1024)(128)(4,1)} %bitcast.316), calls=%async_computation.3 | async-start | bytes 1048576
  389.4 5.6 copy-start.1
  393.6 36.3 %collective-permute-start.10 = (bf16[2,2,2,64,1024]{4,3,1,0,2:T(8,128)(2,1)}, bf16[2,2,2,64,1024]{4,3,1,0,2:T(8,128)(2,1)S(1)}, u32[]{:S(2)}, u32[]{:S(2)}) collective-permute-start(bf16[2,2,2,64,1024]{4,3,1,0,2:T(8,128)(2,1)} %add_convert_fusion.5), channel_id=1, source_target_pairs={{0,4},{1,5},{2,6},{3,7},{4,0},{5,1},{6,2},{7,3},{8,12},{9,13},{10,... | collective-permute-start | bytes 3145736 | tf_op jit(solution)/shard_map/ppermute | solution.py:557
  394.9 4.5 copy-start.3
  398.6 32.7 %collective-permute-start.8 = (bf16[2,2,2,64,1024]{4,3,1,0,2:T(8,128)(2,1)}, bf16[2,2,2,64,1024]{4,3,1,0,2:T(8,128)(2,1)S(1)}, u32[]{:S(2)}, u32[]{:S(2)}) collective-permute-start(bf16[2,2,2,64,1024]{4,3,1,0,2:T(8,128)(2,1)} %add_convert_fusion.6), channel_id=1, source_target_pairs={{0,2},{1,3},{2,0},{3,1},{4,6},{5,7},{6,4},{7,5},{8,10},{9,11},{10,... | collective-permute-start | bytes 3145736 | tf_op jit(solution)/shard_map/ppermute | solution.py:557
  402.9 39.4 %collective-permute-start.17 = (bf16[2,2,2,64,1024]{4,3,1,0,2:T(8,128)(2,1)}, bf16[2,2,2,64,1024]{4,3,1,0,2:T(8,128)(2,1)S(1)}, u32[]{:S(2)}, u32[]{:S(2)}) collective-permute-start(bf16[2,2,2,64,1024]{4,3,1,0,2:T(8,128)(2,1)} %add_convert_fusion.3), channel_id=1, source_target_pairs={{0,4},{1,5},{2,6},{3,7},{4,0},{5,1},{6,2},{7,3},{8,12},{9,13},{10,... | collective-permute-start | bytes 3145736 | tf_op jit(solution)/shard_map/ppermute | solution.py:557
  404.4 4.2 copy-start.5
  408.1 39.2 %collective-permute-start.15 = (bf16[2,2,2,64,1024]{4,3,1,0,2:T(8,128)(2,1)}, bf16[2,2,2,64,1024]{4,3,1,0,2:T(8,128)(2,1)S(1)}, u32[]{:S(2)}, u32[]{:S(2)}) collective-permute-start(bf16[2,2,2,64,1024]{4,3,1,0,2:T(8,128)(2,1)} %add_convert_fusion.4), channel_id=1, source_target_pairs={{0,2},{1,3},{2,0},{3,1},{4,6},{5,7},{6,4},{7,5},{8,10},{9,11},{10,... | collective-permute-start | bytes 3145736 | tf_op jit(solution)/shard_map/ppermute | solution.py:557
  421.2 43.6 %collective-permute-start.24 = (bf16[2,2,2,64,1024]{4,3,1,0,2:T(8,128)(2,1)S(1)}, bf16[2,2,2,64,1024]{4,3,1,0,2:T(8,128)(2,1)}, u32[]{:S(2)}, u32[]{:S(2)}) collective-permute-start(bf16[2,2,2,64,1024]{4,3,1,0,2:T(8,128)(2,1)S(1)} %add_convert_fusion.1), channel_id=1, source_target_pairs={{0,4},{1,5},{2,6},{3,7},{4,0},{5,1},{6,2},{7,3},{8,12},{9,13},{10,... | collective-permute-start | bytes 3145736 | tf_op jit(solution)/shard_map/ppermute | solution.py:557
  427.5 2.5 copy-start.15
  430.0 2.7 copy-start.6
  430.0 2.7 copy-start.12
  430.0 2.7 copy-start.13
  430.0 39.8 %collective-permute-start.22 = (bf16[2,2,2,64,1024]{4,3,1,0,2:T(8,128)(2,1)S(1)}, bf16[2,2,2,64,1024]{4,3,1,0,2:T(8,128)(2,1)S(1)}, u32[]{:S(2)}, u32[]{:S(2)}) collective-permute-start(bf16[2,2,2,64,1024]{4,3,1,0,2:T(8,128)(2,1)S(1)} %copy-done.15), channel_id=1, source_target_pairs={{0,2},{1,3},{2,0},{3,1},{4,6},{5,7},{6,4},{7,5},{8,10},{9,11},{10,... | collective-permute-start | bytes 3145736 | tf_op jit(solution)/shard_map/ppermute | solution.py:557
  431.3 61.0 %collective-permute-start.1 = (bf16[2,2,2,64,1024]{4,3,1,0,2:T(8,128)(2,1)S(1)}, bf16[2,2,2,64,1024]{4,3,1,0,2:T(8,128)(2,1)S(1)}, u32[]{:S(2)}, u32[]{:S(2)}) collective-permute-start(bf16[2,2,2,64,1024]{4,3,1,0,2:T(8,128)(2,1)S(1)} %add_convert_fusion.7), channel_id=1, source_target_pairs={{0,2},{1,3},{2,0},{3,1},{4,6},{5,7},{6,4},{7,5},{8,10},{9,11},{10,... | collective-permute-start | bytes 3145736 | tf_op jit(solution)/shard_map/ppermute | solution.py:557
  432.6 15.5 %copy-start.10 = (bf16[2,2,128,1024]{3,2,1,0:T(8,128)(2,1)S(1)}, bf16[2,2,128,1024]{3,2,1,0:T(8,128)(2,1)}, u32[]{:S(2)}) copy-start(bf16[2,2,128,1024]{3,2,1,0:T(8,128)(2,1)} %get-tuple-element.119) | copy-start | bytes 3145732
  432.6 15.5 %copy-start.11 = (bf16[2,2,128,1024]{3,2,1,0:T(8,128)(2,1)S(1)}, bf16[2,2,128,1024]{3,2,1,0:T(8,128)(2,1)}, u32[]{:S(2)}) copy-start(bf16[2,2,128,1024]{3,2,1,0:T(8,128)(2,1)} %get-tuple-element.120) | copy-start | bytes 3145732
  442.3 87.6 %collective-permute-start.3 = (bf16[2,2,2,80,1024]{4,3,1,0,2:T(8,128)(2,1)S(1)}, bf16[2,2,2,80,1024]{4,3,1,0,2:T(8,128)(2,1)S(1)}, u32[]{:S(2)}, u32[]{:S(2)}) collective-permute-start(bf16[2,2,2,80,1024]{4,3,1,0,2:T(8,128)(2,1)S(1)} %add_convert_fusion), channel_id=1, source_target_pairs={{0,4},{1,5},{2,6},{3,7},{4,0},{5,1},{6,2},{7,3},{8,12},{9,13},{10,... | collective-permute-start | bytes 3932168 | tf_op jit(solution)/shard_map/ppermute | solution.py:557
  447.3 56.8 %collective-permute-start.9 = (bf16[2,2,64,1024]{3,2,1,0:T(8,128)(2,1)}, bf16[2,2,64,1024]{3,2,1,0:T(8,128)(2,1)S(1)}, u32[]{:S(2)}, u32[]{:S(2)}) collective-permute-start(bf16[2,2,64,1024]{3,2,1,0:T(8,128)(2,1)} %get-tuple-element.155), channel_id=1, source_target_pairs={{0,4},{1,5},{2,6},{3,7},{4,0},{5,1},{6,2},{7,3},{8,12},{9,13},{10,... | collective-permute-start | bytes 1572872 | tf_op jit(solution)/shard_map/ppermute | solution.py:557
  448.1 22.5 %copy-start.8 = (bf16[2,2,128,1024]{3,2,1,0:T(8,128)(2,1)S(1)}, bf16[2,2,128,1024]{3,2,1,0:T(8,128)(2,1)}, u32[]{:S(2)}) copy-start(bf16[2,2,128,1024]{3,2,1,0:T(8,128)(2,1)} %get-tuple-element.113) | copy-start | bytes 3145732
  448.1 22.5 %copy-start.9 = (bf16[2,2,128,1024]{3,2,1,0:T(8,128)(2,1)S(1)}, bf16[2,2,128,1024]{3,2,1,0:T(8,128)(2,1)}, u32[]{:S(2)}) copy-start(bf16[2,2,128,1024]{3,2,1,0:T(8,128)(2,1)} %get-tuple-element.114) | copy-start | bytes 3145732
  464.9 40.6 %collective-permute-start.11 = (bf16[2,2,64,1024]{3,2,1,0:T(8,128)(2,1)S(1)}, bf16[2,2,64,1024]{3,2,1,0:T(8,128)(2,1)S(1)}, u32[]{:S(2)}, u32[]{:S(2)}) collective-permute-start(bf16[2,2,64,1024]{3,2,1,0:T(8,128)(2,1)S(1)} %get-tuple-element.160), channel_id=1, source_target_pairs={{0,2},{1,3},{2,0},{3,1},{4,6},{5,7},{6,4},{7,5},{8,10},{9,11},{10,... | collective-permute-start | bytes 1572872 | tf_op jit(solution)/shard_map/ppermute | solution.py:557
  469.8 45.5 %collective-permute-start.16 = (bf16[2,2,64,1024]{3,2,1,0:T(8,128)(2,1)S(1)}, bf16[2,2,64,1024]{3,2,1,0:T(8,128)(2,1)S(1)}, u32[]{:S(2)}, u32[]{:S(2)}) collective-permute-start(bf16[2,2,64,1024]{3,2,1,0:T(8,128)(2,1)S(1)} %get-tuple-element.156), channel_id=1, source_target_pairs={{0,4},{1,5},{2,6},{3,7},{4,0},{5,1},{6,2},{7,3},{8,12},{9,13},{10,... | collective-permute-start | bytes 1572872 | tf_op jit(solution)/shard_map/ppermute | solution.py:557
  492.3 24.5 %collective-permute-start.18 = (bf16[2,2,64,1024]{3,2,1,0:T(8,128)(2,1)S(1)}, bf16[2,2,64,1024]{3,2,1,0:T(8,128)(2,1)S(1)}, u32[]{:S(2)}, u32[]{:S(2)}) collective-permute-start(bf16[2,2,64,1024]{3,2,1,0:T(8,128)(2,1)S(1)} %get-tuple-element.159), channel_id=1, source_target_pairs={{0,2},{1,3},{2,0},{3,1},{4,6},{5,7},{6,4},{7,5},{8,10},{9,11},{10,... | collective-permute-start | bytes 1572872 | tf_op jit(solution)/shard_map/ppermute | solution.py:557
  504.1 22.5 %collective-permute-start.23 = (bf16[2,2,64,1024]{3,2,1,0:T(8,128)(2,1)S(1)}, bf16[2,2,64,1024]{3,2,1,0:T(8,128)(2,1)S(1)}, u32[]{:S(2)}, u32[]{:S(2)}) collective-permute-start(bf16[2,2,64,1024]{3,2,1,0:T(8,128)(2,1)S(1)} %get-tuple-element.157), channel_id=1, source_target_pairs={{0,4},{1,5},{2,6},{3,7},{4,0},{5,1},{6,2},{7,3},{8,12},{9,13},{10,... | collective-permute-start | bytes 1572872 | tf_op jit(solution)/shard_map/ppermute | solution.py:557
  505.5 23.0 %collective-permute-start.25 = (bf16[2,2,64,1024]{3,2,1,0:T(8,128)(2,1)S(1)}, bf16[2,2,64,1024]{3,2,1,0:T(8,128)(2,1)S(1)}, u32[]{:S(2)}, u32[]{:S(2)}) collective-permute-start(bf16[2,2,64,1024]{3,2,1,0:T(8,128)(2,1)S(1)} %get-tuple-element.158), channel_id=1, source_target_pairs={{0,2},{1,3},{2,0},{3,1},{4,6},{5,7},{6,4},{7,5},{8,10},{9,11},{10,... | collective-permute-start | bytes 1572872 | tf_op jit(solution)/shard_map/ppermute | solution.py:557
  515.3 72.6 %collective-permute-start.2 = (bf16[2,2,64,1024]{3,2,1,0:T(8,128)(2,1)S(1)}, bf16[2,2,64,1024]{3,2,1,0:T(8,128)(2,1)S(1)}, u32[]{:S(2)}, u32[]{:S(2)}) collective-permute-start(bf16[2,2,64,1024]{3,2,1,0:T(8,128)(2,1)S(1)} %get-tuple-element.161), channel_id=1, source_target_pairs={{0,4},{1,5},{2,6},{3,7},{4,0},{5,1},{6,2},{7,3},{8,12},{9,13},{10,... | collective-permute-start | bytes 1572872 | tf_op jit(solution)/shard_map/ppermute | solution.py:557
  516.8 46.4 %collective-permute-start.12 = (bf16[2,128,1024]{2,1,0:T(8,128)(2,1)S(1)}, bf16[2,128,1024]{2,1,0:T(8,128)(2,1)S(1)}, u32[]{:S(2)}, u32[]{:S(2)}) collective-permute-start(bf16[2,128,1024]{2,1,0:T(8,128)(2,1)S(1)} %pad_maximum_fusion.5), channel_id=1, source_target_pairs={{0,16},{1,17},{2,18},{3,19},{4,20},{5,21},{6,22},{7,23},{8,24},{9,... | collective-permute-start | bytes 1572872 | tf_op jit(solution)/shard_map/ppermute | solution.py:557
  526.6 47.9 %collective-permute-start.19 = (bf16[2,128,1024]{2,1,0:T(8,128)(2,1)S(1)}, bf16[2,128,1024]{2,1,0:T(8,128)(2,1)S(1)}, u32[]{:S(2)}, u32[]{:S(2)}) collective-permute-start(bf16[2,128,1024]{2,1,0:T(8,128)(2,1)S(1)} %pad_maximum_fusion.6), channel_id=1, source_target_pairs={{0,16},{1,17},{2,18},{3,19},{4,20},{5,21},{6,22},{7,23},{8,24},{9,... | collective-permute-start | bytes 1572872 | tf_op jit(solution)/shard_map/ppermute | solution.py:557
  528.5 1.5 copy-start.7
  528.7 56.0 %collective-permute-start.26 = (bf16[2,128,1024]{2,1,0:T(8,128)(2,1)S(1)}, bf16[2,128,1024]{2,1,0:T(8,128)(2,1)S(1)}, u32[]{:S(2)}, u32[]{:S(2)}) collective-permute-start(bf16[2,128,1024]{2,1,0:T(8,128)(2,1)S(1)} %pad_maximum_fusion.8), channel_id=1, source_target_pairs={{0,16},{1,17},{2,18},{3,19},{4,20},{5,21},{6,22},{7,23},{8,24},{9,... | collective-permute-start | bytes 1572872 | tf_op jit(solution)/shard_map/ppermute | solution.py:557
  530.8 65.9 %collective-permute-start.4 = (bf16[2,2,80,1024]{3,2,1,0:T(8,128)(2,1)S(1)}, bf16[2,2,80,1024]{3,2,1,0:T(8,128)(2,1)S(1)}, u32[]{:S(2)}, u32[]{:S(2)}) collective-permute-start(bf16[2,2,80,1024]{3,2,1,0:T(8,128)(2,1)S(1)} %get-tuple-element.153), channel_id=1, source_target_pairs={{0,2},{1,3},{2,0},{3,1},{4,6},{5,7},{6,4},{7,5},{8,10},{9,11},{10,... | collective-permute-start | bytes 1966088 | tf_op jit(solution)/shard_map/ppermute | solution.py:557
  563.3 27.6 %collective-permute-start.13 = (bf16[128,1024]{1,0:T(8,128)(2,1)S(1)}, bf16[128,1024]{1,0:T(8,128)(2,1)S(1)}, u32[]{:S(2)}, u32[]{:S(2)}) collective-permute-start(bf16[128,1024]{1,0:T(8,128)(2,1)S(1)} %fusion.53), channel_id=1, source_target_pairs={{0,8},{1,9},{2,10},{3,11},{4,12},{5,13},{6,14},{7,15},{8,0},{9,1},... | collective-permute-start | bytes 786440 | tf_op jit(solution)/shard_map/ppermute | solution.py:557
  574.6 22.0 %collective-permute-start.20 = (bf16[128,1024]{1,0:T(8,128)(2,1)S(1)}, bf16[128,1024]{1,0:T(8,128)(2,1)S(1)}, u32[]{:S(2)}, u32[]{:S(2)}) collective-permute-start(bf16[128,1024]{1,0:T(8,128)(2,1)S(1)} %fusion.56), channel_id=1, source_target_pairs={{0,8},{1,9},{2,10},{3,11},{4,12},{5,13},{6,14},{7,15},{8,0},{9,1},... | collective-permute-start | bytes 786440 | tf_op jit(solution)/shard_map/ppermute | solution.py:557
  584.8 43.5 %collective-permute-start.27 = (bf16[128,1024]{1,0:T(8,128)(2,1)S(1)}, bf16[128,1024]{1,0:T(8,128)(2,1)S(1)}, u32[]{:S(2)}, u32[]{:S(2)}) collective-permute-start(bf16[128,1024]{1,0:T(8,128)(2,1)S(1)} %fusion.59), channel_id=1, source_target_pairs={{0,8},{1,9},{2,10},{3,11},{4,12},{5,13},{6,14},{7,15},{8,0},{9,1},... | collective-permute-start | bytes 786440 | tf_op jit(solution)/shard_map/ppermute | solution.py:557
  596.9 27.6 %collective-permute-start.5 = (bf16[2,144,1024]{2,1,0:T(8,128)(2,1)S(1)}, bf16[2,144,1024]{2,1,0:T(8,128)(2,1)S(1)}, u32[]{:S(2)}, u32[]{:S(2)}) collective-permute-start(bf16[2,144,1024]{2,1,0:T(8,128)(2,1)S(1)} %pad_maximum_fusion.1), channel_id=1, source_target_pairs={{0,16},{1,17},{2,18},{3,19},{4,20},{5,21},{6,22},{7,23},{8,24},{9,... | collective-permute-start | bytes 1769480 | tf_op jit(solution)/shard_map/ppermute | solution.py:557
  624.6 10.0 %collective-permute-start.6 = (bf16[144,1024]{1,0:T(8,128)(2,1)S(1)}, bf16[144,1024]{1,0:T(8,128)(2,1)S(1)}, u32[]{:S(2)}, u32[]{:S(2)}) collective-permute-start(bf16[144,1024]{1,0:T(8,128)(2,1)S(1)} %fusion.49), channel_id=1, source_target_pairs={{0,8},{1,9},{2,10},{3,11},{4,12},{5,13},{6,14},{7,15},{8,0},{9,1},... | collective-permute-start | bytes 884744 | tf_op jit(solution)/shard_map/ppermute | solution.py:557
Sparse Core Ops, SparseCore 0:
  15.8 118.7 all-gather.2
  138.0 113.1 all-gather.4

commit v2 on v1

--- a/solution.py
+++ b/solution.py
@@ -470,17 +470,6 @@
         target[j // 2, at : at + size, :] = rows.astype(BF16)
 
 
-def outer_body(me, act, go, keep, send, held):
-    held[...] = tn(act[...], go[...])
-    place(keep, send, 0, 128, lambda d: held[pl.ds(pl.multiple_of(d * 128, 128), 128), :], me[0])
-
-
-def inner_body(me, low, gi, keep, send, held):
-    for part in range(4):
-        held[...] = tn(low[...], gi[:, part * 1024 : part * 1024 + 1024])
-        place(keep, send, part * 32, 32, lambda d: held[pl.ds(pl.multiple_of(d * 32, 32), 32), :], me[0])
-
-
 def group_of(step, me):
     return lax.bitwise_xor(step, lax.div(me[0], 8))
 
@@ -491,26 +480,34 @@
     return out, spec
 
 
-def outer_weights(me, act, go):
+def ffn_weights_body(act, go, low, gi, out):
+    step = pl.program_id(0)
+    width = go.shape[1]
+
+    @pl.when(step < 4)
+    def _():
+        out[...] = tn(act[...], go[...]).astype(BF16).reshape(8, 128, width)
+
+    @pl.when(step >= 4)
+    def _():
+        for part in range(4):
+            rows = tn(low[...], gi[:, part * 1024 : part * 1024 + 1024]).astype(BF16)
+            out[:, part * 32 : part * 32 + 32, :] = rows.reshape(8, 32, width)
+
+
+def ffn_weights(act, go, low, gi):
     count, width = go.shape
-    out, spec = payload(128, width)
-    return call(
-        outer_body, "outer_weights", out, (4,),
-        [pl.BlockSpec((count, 1024), lambda i, me: (0, group_of(i, me))), full(go.shape)],
-        spec, [pltpu.VMEM((1024, width), F32)], 1,
-        flops=8 * count * width * width, moved=11 * MIB,
-    )(me, act, go)
-
-
-def inner_weights(me, low, gi):
-    count, width = low.shape
-    out, spec = payload(128, width)
-    return call(
-        inner_body, "inner_weights", out, (4,),
-        [pl.BlockSpec((count, 256), lambda i, me: (0, group_of(i, me))), full(gi.shape)],
-        spec, [pltpu.VMEM((256, width), F32)], 1,
-        flops=8 * count * width * width, moved=11 * MIB,
-    )(me, low, gi)
+    return call(
+        ffn_weights_body, "ffn_weights", shape((BLOCKS, 256, width), BF16), (8,),
+        [
+            pl.BlockSpec((count, 1024), lambda i: (0, jnp.minimum(i, 3))),
+            full(go.shape),
+            pl.BlockSpec((count, 256), lambda i: (0, jnp.maximum(i - 4, 0))),
+            full(gi.shape),
+        ],
+        pl.BlockSpec((8, 128, width), lambda i: (lax.rem(i, 4), lax.div(i, 4), 0)),
+        flops=16 * count * width * width, moved=22 * MIB,
+    )(act, go, low, gi)
 
 
 def square_body(me, *refs):
@@ -532,12 +529,12 @@
     def pieces(d):
         return pltpu.roll(rows, lax.rem(width - (step * 8 + d) * 32, width), 1)
 
-    place(keep, send, 128, 16, pieces, me[0])
+    place(keep, send, 128, 32, pieces, me[0])
 
 
 def square_weights(me, pairs, name, vecs=None):
     width = pairs[0][0].shape[1]
-    out, spec = payload(128 if vecs is None else 144, width)
+    out, spec = payload(128 if vecs is None else 160, width)
     ins, operands, flops = [], [], 0
     for rows, grads in pairs:
         ins.append(pl.BlockSpec((rows.shape[0], 256), lambda i, me: (0, group_of(i, me))))
@@ -553,46 +550,196 @@
     )(me, *operands)
 
 
-def swap(rows, distance):
-    return lax.ppermute(rows, "dp", [(i, i ^ distance) for i in range(BLOCKS)])
-
-
-def scatter_sum(keep, send):
-    rows, width = keep.shape[1:]
-    cut = (rows // 32) * 16
-    came = swap(send, 1)
-    dims = (2, 2, 2, 2, rows, width)
-    keep, came = keep.reshape(dims), came.reshape(dims)
-
-    def start(index, part):
-        return keep[index][..., part, :].astype(F32) + came[index][..., part, :].astype(F32)
-
-    a, b = slice(0, cut), slice(cut, rows)
+def flip(me, bit):
+    return me + bit - 2 * bit * lax.rem(lax.div(me, bit), 2)
+
+def send(src, dst, out_sem, in_sem, to):
+    return pltpu.make_async_remote_copy(src_ref=src, dst_ref=dst, send_sem=out_sem, recv_sem=in_sem, device_id=(to,), device_id_type=pl.DeviceIdType.MESH)
+
+def greet(me, bits):
+    barrier = pltpu.get_barrier_semaphore()
+    for bit in bits:
+        pl.semaphore_signal(barrier, inc=1, device_id=(flip(me, bit),), device_id_type=pl.DeviceIdType.MESH)
+    pl.semaphore_wait(barrier, len(bits))
+
+PAIR=32; HALF=16
+CORE,XB,YB,NEAR,FAR=1,2,4,8,16
+
+def gather_body(own, g, local_sem, out_sem, in_sem):
+    me = lax.axis_index("dp").astype(jnp.int32)
+    c, x, y, zl, zh = [lax.rem(lax.div(me, b), 2) for b in (1, 2, 4, 8, 16)]
+    ticks = own.shape[0] // PAIR
     every = slice(None)
-    a_came = swap(start((every, every, every, 1), a).astype(BF16), 2)
-    b_came = swap(start((every, every, 1), b).astype(BF16), 4)
-
-    def a_second(at):
-        return start((every, every, at, 0), a) + a_came[:, :, at].astype(F32)
-
-    def b_second(at):
-        return start((every, every, 0, at), b) + b_came[:, :, at].astype(F32)
-
-    a_more = swap(a_second(1).astype(BF16), 4)
-    b_more = swap(b_second(1).astype(BF16), 2)
-
-    def third(at):
-        return jnp.concatenate(
-            [a_second(0)[at] + a_more[at].astype(F32), b_second(0)[at] + b_more[at].astype(F32)], axis=-2
-        )
-
-    far = swap(third(1).astype(BF16), 16)
-
-    def fourth(at):
-        return third(0)[at] + far[at].astype(F32)
-
-    near = swap(fourth(1).astype(BF16), 8)
-    return fourth(0) + near.astype(F32)
+    greet(me, (CORE, XB, YB, NEAR, FAR))
+
+    def rows(p): return pl.ds(pl.multiple_of(p * PAIR, PAIR), PAIR)
+    def half(p, k): return pl.ds(pl.multiple_of(p * PAIR + k * HALF, HALF), HALF)
+    def local(p): return pltpu.make_async_copy(own.at[rows(p)], g.at[zh, zl, y, x, c, rows(p)], local_sem.at[p])
+    def same(ref, k, p, bit):
+        return send(ref, ref, out_sem.at[k, p], in_sem.at[k, p], flip(me, bit))
+    def near(p):
+        return send(own.at[rows(p)], g.at[zh, zl, y, x, c, rows(p)], out_sem.at[0, p], in_sem.at[0, p], flip(me, NEAR))
+    def far(p): return same(g.at[zh, every, y, x, c, rows(p)], 1, p, FAR)
+    def a1(p): return same(g.at[every, every, y, x, c, half(p, 0)], 2, p, XB)
+    def b1(p): return same(g.at[every, every, y, x, c, half(p, 1)], 3, p, YB)
+    def a2(p): return same(g.at[every, every, y, every, c, half(p, 0)], 4, p, YB)
+    def b2(p): return same(g.at[every, every, every, x, c, half(p, 1)], 5, p, XB)
+    def core(p): return same(g.at[every, every, every, every, c, rows(p)], 6, p, CORE)
+
+    def tick(t, _):
+        @pl.when(t < ticks)
+        def _():
+            local(t).start()
+            near(t).start()
+        @pl.when((t >= 1) & (t < ticks + 1))
+        def _():
+            p = t - 1
+            local(p).wait()
+            near(p).wait_recv()
+            far(p).start()
+        @pl.when((t >= 2) & (t < ticks + 2))
+        def _():
+            p = t - 2
+            far(p).wait_recv()
+            a1(p).start()
+            b1(p).start()
+        @pl.when((t >= 3) & (t < ticks + 3))
+        def _():
+            p = t - 3
+            a1(p).wait_recv()
+            a2(p).start()
+            b1(p).wait_recv()
+            b2(p).start()
+        @pl.when((t >= 4) & (t < ticks + 4))
+        def _():
+            p = t - 4
+            a2(p).wait_recv()
+            b2(p).wait_recv()
+            core(p).start()
+        return 0
+    lax.fori_loop(0, ticks + 4, tick, 0)
+    def close(p, _):
+        core(p).wait_recv()
+        for copy in (near, far, a1, b1, a2, b2, core):
+            copy(p).wait_send()
+        return 0
+    lax.fori_loop(0, ticks, close, 0)
+
+def gather_rows(own):
+    ticks = own.shape[0] // PAIR
+    out = pl.pallas_call(
+        gather_body,
+        out_shape=jax.ShapeDtypeStruct((2,2,2,2,2)+own.shape, own.dtype),
+        in_specs=[pl.BlockSpec(memory_space=pl.ANY)],
+        out_specs=pl.BlockSpec(memory_space=pl.ANY),
+        scratch_shapes=[pltpu.SemaphoreType.DMA((ticks,)), pltpu.SemaphoreType.DMA((7, ticks)), pltpu.SemaphoreType.DMA((7, ticks))],
+        compiler_params=pltpu.CompilerParams(collective_id=0, has_side_effects=True, vmem_limit_bytes=40*MIB),
+        name="gather_rows",
+    )(own)
+    return out.reshape((BLOCKS,)+own.shape)
+
+def scatter_body(count, *refs):
+    pays = [(refs[2*i], refs[2*i+1]) for i in range(count)]
+    out, keep, came0, put1, came1, put2, came2, put3, came3, put4, came4, load_sem, out_sem, in_sem = refs[2*count:]
+    me = lax.axis_index("dp").astype(jnp.int32)
+    ticks = keep.shape[0]
+    greet(me, (CORE, XB, YB, NEAR, FAR))
+    first = []
+    p = 0
+    for kept, sent in pays:
+        for at in range(0, kept.shape[1], PAIR):
+            load = pltpu.make_async_copy(kept.at[:, pl.ds(at, PAIR)], keep.at[p], load_sem.at[p])
+            load.start()
+            put = send(sent.at[:, pl.ds(at, PAIR)], came0.at[p], out_sem.at[0, p], in_sem.at[0, p], flip(me, CORE))
+            put.start()
+            first.append(put)
+            p += 1
+    def loaded(p): return pltpu.make_async_copy(pays[0][0].at[:, pl.ds(0, PAIR)], keep.at[p], load_sem.at[p])
+    def swap0(p): return send(pays[0][1].at[:, pl.ds(0, PAIR)], came0.at[p], out_sem.at[0, p], in_sem.at[0, p], flip(me, CORE))
+    def a1(p): return send(put1.at[p, 0], came1.at[p, 0], out_sem.at[1, p], in_sem.at[1, p], flip(me, XB))
+    def b1(p): return send(put1.at[p, 1], came1.at[p, 1], out_sem.at[2, p], in_sem.at[2, p], flip(me, YB))
+    def a2(p): return send(put2.at[p, 0], came2.at[p, 0], out_sem.at[3, p], in_sem.at[3, p], flip(me, YB))
+    def b2(p): return send(put2.at[p, 1], came2.at[p, 1], out_sem.at[4, p], in_sem.at[4, p], flip(me, XB))
+    def far(p): return send(put3.at[p], came3.at[p], out_sem.at[5, p], in_sem.at[5, p], flip(me, FAR))
+    def near(p): return send(put4.at[p], came4.at[p], out_sem.at[6, p], in_sem.at[6, p], flip(me, NEAR))
+    def base(p, block, h):
+        cut = slice(h * HALF, h * HALF + HALF)
+        return keep[p, block, cut, :].astype(F32) + came0[p, block, cut, :].astype(F32)
+    def second(p, z, other, h):
+        block = z * 4 + (other * 2 if h == 0 else other)
+        return base(p, block, h) + came1[p, h, z * 2 + other].astype(F32)
+    def third(p, z, h):
+        return second(p, z, 0, h) + came2[p, h, z].astype(F32)
+    def fourth(p, zl, h):
+        return third(p, zl, h) + came3[p, zl, h * HALF : h * HALF + HALF, :].astype(F32)
+    def tick(t, _):
+        @pl.when(t < ticks)
+        def _():
+            p = t
+            loaded(p).wait()
+            swap0(p).wait_recv()
+            for z in range(4):
+                for other in range(2):
+                    put1[p, 0, z * 2 + other] = base(p, z * 4 + other * 2 + 1, 0).astype(BF16)
+            a1(p).start()
+            for z in range(4):
+                for other in range(2):
+                    put1[p, 1, z * 2 + other] = base(p, z * 4 + 2 + other, 1).astype(BF16)
+            b1(p).start()
+        @pl.when((t >= 1) & (t < ticks + 1))
+        def _():
+            p = t - 1
+            a1(p).wait_recv()
+            for z in range(4): put2[p, 0, z] = second(p, z, 1, 0).astype(BF16)
+            a2(p).start()
+            b1(p).wait_recv()
+            for z in range(4): put2[p, 1, z] = second(p, z, 1, 1).astype(BF16)
+            b2(p).start()
+        @pl.when((t >= 2) & (t < ticks + 2))
+        def _():
+            p = t - 2
+            a2(p).wait_recv()
+            b2(p).wait_recv()
+            for zl in range(2):
+                for h in range(2):
+                    put3[p, zl, h * HALF : h * HALF + HALF, :] = third(p, 2 + zl, h).astype(BF16)
+            far(p).start()
+        @pl.when((t >= 3) & (t < ticks + 3))
+        def _():
+            p = t - 3
+            far(p).wait_recv()
+            for h in range(2): put4[p, h * HALF : h * HALF + HALF, :] = fourth(p, 1, h).astype(BF16)
+            near(p).start()
+        @pl.when(t >= 4)
+        def _():
+            p = t - 4
+            near(p).wait_recv()
+            for h in range(2):
+                at = pl.ds(pl.multiple_of(p * PAIR + h * HALF, HALF), HALF)
+                out[at, :] = fourth(p, 0, h) + came4[p, h * HALF : h * HALF + HALF, :].astype(F32)
+        return 0
+    lax.fori_loop(0, ticks + 4, tick, 0)
+    def close(p, _):
+        for copy in (swap0, a1, b1, a2, b2, far, near):
+            copy(p).wait_send()
+        return 0
+    lax.fori_loop(0, ticks, close, 0)
+
+def scatter_rows(pays):
+    ticks = sum(k.shape[1] for k, _ in pays) // PAIR
+    width = pays[0][0].shape[2]
+    v = lambda *s: pltpu.VMEM((ticks,)+s+(width,), BF16)
+    flat = [a for p in pays for a in p]
+    return pl.pallas_call(
+        functools.partial(scatter_body, len(pays)),
+        out_shape=jax.ShapeDtypeStruct((ticks * PAIR, width), F32),
+        in_specs=[pl.BlockSpec(memory_space=pl.ANY)] * len(flat),
+        out_specs=pl.BlockSpec(memory_space=pltpu.VMEM),
+        scratch_shapes=[v(16, PAIR), v(16, PAIR), v(2, 8, HALF), v(2, 8, HALF), v(2, 4, HALF), v(2, 4, HALF), v(2, PAIR), v(2, PAIR), v(PAIR), v(PAIR),
+            pltpu.SemaphoreType.DMA((ticks,)), pltpu.SemaphoreType.DMA((7, ticks)), pltpu.SemaphoreType.DMA((7, ticks))],
+        compiler_params=pltpu.CompilerParams(collective_id=1, has_side_effects=True, vmem_limit_bytes=60*MIB),
+        name="scatter_rows",
+    )(*flat)
 
 
 def absolute(keep, send):
@@ -602,7 +749,7 @@
 def pack_vectors(vectors, devices):
     own = vectors[0].shape[0]
     rows = jnp.stack(vectors)
-    return jnp.pad(rows, ((0, 16 - len(vectors)), (0, 1024 - own)))
+    return jnp.pad(rows, ((0, 32 - len(vectors)), (0, 1024 - own)))
 
 
 def gather(rows):
@@ -623,11 +770,10 @@
     if direct:
         me = lax.axis_index("dp").astype(jnp.int32).reshape(1)
         pack = jnp.concatenate(squares + [pack_vectors(vectors, devices)], axis=0)
-        stack = gather(pack).reshape(BLOCKS, -1, width)
+        stack = gather_rows(pack)
         vecs = stack[:, 256:264, :32].transpose(1, 0, 2).reshape(8, width).astype(F32)
         parts = [outer_weight] + [inner_weight[:, i : i + width] for i in range(0, hidden, width)]
         pack = jnp.concatenate(parts, axis=0)
-        pack, _ = lax.optimization_barrier((pack, stack[0, :1]))
         wide = gather(pack).reshape(BLOCKS, -1, width)
     else:
         me = jnp.zeros((1,), jnp.int32)
@@ -645,9 +791,8 @@
     cross_mixture, cross_lse = cross_forward(memory_lengths, cross_q, keys, values)
     second_sum, second, second_low = second_norm(cross_mixture, stack, 7, first_out, vecs)
     act, slope, output_rows, gts, go, third_grads = ffn_forward(second_low, second, wide, cotangent, vecs)
-    outer_pay = outer_weights(me, act, go)
     gi, gss, gci, gcm, second_grads = ffn_backward(go, gts, slope, wide, second_sum, stack, 7, vecs)
-    inner_pay = inner_weights(me, second_low, gi)
+    ffn_pay = ffn_weights(act, go, second_low, gi)
     dq, dk, dv = cross_backward(memory_lengths, cross_q, keys, values, gcm, cross_mixture, cross_lse)
     cross_pay = square_weights(
         me, [(first_low, dq), (memory, dk), (memory, dv), (cross_mixture, gci)], "cross_weights"
@@ -655,32 +800,31 @@
     gfs, gsi, gq, gk, gv, first_grads = self_backward(
         target_lengths, gss, dq, stack, 6, 5, first_sum, vecs, q, k, v, mixture, lse
     )
-    grads = jnp.concatenate([first_grads[:2], second_grads[:2], third_grads[:2], jnp.zeros((10, width), F32)])
+    grads = jnp.concatenate([first_grads[:2], second_grads[:2], third_grads[:2], jnp.zeros((26, width), F32)])
     self_pay = square_weights(me, [(tokens, gq), (tokens, gk), (tokens, gv), (mixture, gsi)], "self_weights", grads)
     memory_grad = memory_gradient(dk, dv, stack, 0, 1)
     tokens_grad = tokens_gradient(gfs, gq, gk, gv, stack, (2, 3, 4))
 
     if direct:
-        outer_own = scatter_sum(*outer_pay)
-        inner_own = scatter_sum(*inner_pay)
-        cross_own = scatter_sum(*cross_pay)
-        self_own = scatter_sum(*self_pay)
-        inner_own = jnp.concatenate([inner_own[i : i + 32] for i in range(0, 128, 32)], axis=1)
-        cross_own = [cross_own[i : i + 32] for i in range(0, 128, 32)]
-        vec_own = [self_own[128 + i, :32] for i in range(6)]
-        self_own = [self_own[i : i + 32] for i in range(0, 128, 32)]
+        ffn_own = lax.psum_scatter(ffn_pay.reshape(-1, width), "dp", scatter_dimension=0, tiled=True).astype(F32)
+        outer_own = ffn_own[:128]
+        inner_own = jnp.concatenate([ffn_own[i : i + 32] for i in range(128, 256, 32)], axis=1)
+        owned = scatter_rows([cross_pay, self_pay])
+        cross_own = [owned[i : i + 32] for i in range(0, 128, 32)]
+        self_own = [owned[i : i + 32] for i in range(128, 256, 32)]
+        vec_own = [owned[256 + i, :32] for i in range(6)]
     else:
-        def owned(rows):
+        def summed(rows):
             return lax.psum_scatter(rows.astype(F32), "dp", scatter_dimension=0, tiled=True)
 
-        outer_own = owned(absolute(*outer_pay).reshape(-1, width))
-        inner_rows = absolute(*inner_pay)
-        inner_rows = jnp.concatenate([inner_rows[:, i : i + 32].reshape(-1, width) for i in range(0, 128, 32)], axis=1)
-        inner_own = owned(inner_rows)
+        outer_own = summed(ffn_pay[:, :128].reshape(-1, width))
+        inner_own = summed(
+            jnp.concatenate([ffn_pay[:, i : i + 32].reshape(-1, width) for i in range(128, 256, 32)], axis=1)
+        )
         cross_rows, self_rows = absolute(*cross_pay), absolute(*self_pay)
-        cross_own = [owned(cross_rows[:, i : i + 32].reshape(-1, width)) for i in range(0, 128, 32)]
-        self_own = [owned(self_rows[:, i : i + 32].reshape(-1, width)) for i in range(0, 128, 32)]
-        vec_own = [owned(grads[i]) for i in range(6)]
+        cross_own = [summed(cross_rows[:, i : i + 32].reshape(-1, width)) for i in range(0, 128, 32)]
+        self_own = [summed(self_rows[:, i : i + 32].reshape(-1, width)) for i in range(0, 128, 32)]
+        vec_own = [summed(grads[i]) for i in range(6)]
 
     return (
         output_rows, tokens_grad, memory_grad,

time: 653 us -> 546 us (0.84)
  waiting for transfers between devices: 343 us -> 0.04 us
  Pallas kernels: 172 us -> 504 us
  starting transfers between devices: 36.7 us -> 0.08 us
  local copies, waits for them, and re-layouts: 52.3 us -> 20 us
  other arithmetic: 22.7 us -> 2.41 us
    pallas_call x2 -> x3, Pallas kernels: 14.2 us -> 347 us  [the longest x1 193 us: scatter_rows(): pl.pallas_call(functools.partial(scatter_body, len(pays)), out_shape=jax....]
    all_gather x2 -> x1, waiting for transfers between devices: 183 us -> 0.01 us  [gather(): return lax.all_gather(rows, 'dp', axis=0, tiled=True)]
    ppermute x28 -> x0, waiting for transfers between devices: 160 us -> none  [swap(): return lax.ppermute(rows, 'dp', [(i, i ^ distance) for i in range(BLOCKS)])]
    ppermute x28 -> x0, starting transfers between devices: 36.6 us -> none  [swap(): return lax.ppermute(rows, 'dp', [(i, i ^ distance) for i in range(BLOCKS)])]
    squeeze x17 -> x1, local copies, waits for them, and re-layouts: 34.5 us -> 0.53 us  [on_device(): vec_own = [owned[256 + i, :32] for i in range(6)]]
    convert_element_type x14 -> x0, other arithmetic: 11.2 us -> none  [the longest x4 4.68 us: scatter_sum(): a_came = swap(start((every, every, every, 1), a).astype(BF16), 2)]
    add x15 -> x0, other arithmetic: 8.94 us -> none  [the longest x3 6.55 us: b_second(): return start((every, every, 0, at), b) + b_came[:, :, at].astype(F32)]
  transfers between devices with their start and end apart: 30 -> 2, of which waited for: 17 -> 0; matrix products, arithmetic and copies ran while one was open for 10% -> 3% of each run, Pallas kernels for 16% -> 86%
where the time goes in v2:
time: 546 us; the launch traced here: 543 us
  Pallas kernels  504 us (92%)
  local copies, waits for them, and re-layouts  20 us (4%)
  between operations  15.5 us (3%)
    pallas_call x1, Pallas kernels, scatter_rows(): pl.pallas_call(functools.partial(scatter_body, len(pays)), out_shape=jax....  193 us
    pallas_call x1, Pallas kernels, gather_rows(): pl.pallas_call(gather_body, out_shape=jax.ShapeDtypeStruct((2, 2, 2, 2, 2...  142 us
    pallas_call x1, Pallas kernels, cross_backward(): call(cross_back_body, 'cross_backward', [shape(q.shape, BF16), shape(k.sh...  26.3 us
    pallas_call x2, Pallas kernels, square_weights(): call(square_body if vecs is None else square_vec_body, name, out, (4,), i...  25.5 us
    pallas_call x1, Pallas kernels, cross_forward(): call(cross_body, 'cross_forward', [shape(q.shape, BF16), shape((pairs, 8,...  20 us
    pallas_call x1, Pallas kernels, ffn_backward(): call(ffn_back_body, 'ffn_backward', [shape((count, 4096), BF16), shape(go...  14.4 us
    pallas_call x1, Pallas kernels, memory_gradient(): call(memory_grad_body, 'memory_grad', shape(dk.shape, F32), (count // til...  13.8 us
    pallas_call x1, Pallas kernels, ffn_forward(): call(ffn_body, 'ffn_forward', [shape((count, 4096), BF16), shape((count,...  13.7 us
  transfers between devices with their start and end apart: 2, of which 0 were waited for; matrix products, arithmetic and copies ran while one was open for 3% of the time, Pallas kernels for 86%

profile of v2, /device:TPU:14, one launch (start us, length us, event | category | flops | bytes accessed | tf_op | source)
XLA Modules:
  0.0 542.5 jit_solution(8866764790272867308)
XLA Ops:
  7.2 0.0 all-gather.2.cloned.1.call-start
  7.2 1.0 constant_dynamic-update-slice_fusion.8
  8.2 0.8 slice_dynamic-update-slice_fusion.3
  9.1 0.8 slice_dynamic-update-slice_fusion.2
  9.9 0.8 slice_dynamic-update-slice_fusion.1
  10.7 0.8 slice_dynamic-update-slice_fusion
  11.6 0.0 copy-start.1
  11.6 0.8 copy-done.1
  12.4 0.0 all-gather.2.cloned.1.call-update
  12.4 0.0 reduce-scatter.2.cloned.1.call-start
  12.5 0.8 stack.27
  13.2 0.8 constant_dynamic-update-slice_fusion.7
  14.1 0.8 constant_dynamic-update-slice_fusion.6
  14.9 0.8 constant_dynamic-update-slice_fusion.5
  15.8 0.8 constant_dynamic-update-slice_fusion.4
  16.6 0.8 constant_dynamic-update-slice_fusion.3
  17.4 0.8 constant_dynamic-update-slice_fusion.2
  18.3 0.8 constant_dynamic-update-slice_fusion.1
  19.1 0.8 constant_dynamic-update-slice_fusion
  20.0 142.1 %gather_rows.1 = bf16[2,2,2,2,2,288,1024]{6,5,4,3,2,1,0:T(8,128)(2,1)} custom-call(bf16[288,1024]{1,0:T(8,128)(2,1)S(1)} %pad_dynamic-update-slice_fusion.own), custom_call_target="tpu_custom_call" | custom-call | tf_op jit(solution)/shard_map/gather_rows/pallas_call | solution.py:630
  162.1 0.9 convert_bitcast_fusion
  163.0 0.7 reshape.57.vecs
  165.0 10.1 %self_forward.1 = (bf16[256,1024]{1,0:T(8,128)(2,1)}, bf16[256,1024]{1,0:T(8,128)(2,1)}, bf16[256,1024]{1,0:T(8,128)(2,1)}, bf16[256,1024]{1,0:T(8,128)(2,1)}, f...) custom-call(s32[1]{0:T(128)S(6)} %copy.53.length, ...), custom_call_target="tpu_custom_call" | custom-call | flops 2684354560 | bytes 16777216 | tf_op jit(solution)/shard_map/self_forward/pallas_call | solution.py:198
  175.2 13.2 %cross_kv.1 = (bf16[2048,1024]{1,0:T(8,128)(2,1)}, bf16[2048,1024]{1,0:T(8,128)(2,1)}) custom-call(bf16[2048,1024]{1,0:T(8,128)(2,1)} %refs_4_.2, bf16[32,288,1024]{2,1,0:T(8,128)(2,1)} %bitcast.30, bf16[32,288,1024]{2,1,0:T(8,128)(2,1)} %bitcast.31), custom_call_target="tpu_custom_call" | custom-call | flops 8589934592 | bytes 16777216 | tf_op jit(solution)/shard_map/cross_kv/pallas_call | solution.py:154
  188.4 20.0 %cross_forward.1 = (bf16[256,1024]{1,0:T(8,128)(2,1)}, f32[8,8,256]{2,1,0:T(8,128)}) custom-call(s32[1]{0:T(128)S(6)} %copy.54.length, bf16[256,1024]{1,0:T(8,128)(2,1)} %get-tuple-element.59.q, bf16[2048,1024]{1,0:T(8,128)(2,1)} %get-tuple-element.60.k, bf16[2048,1024]{1,0:T(8,128)(2,1)} %get-tuple-element.61.v), custom_call_target="tpu_custom_call" | custom-call | flops 8589934592 | bytes 10485760 | tf_op jit(solution)/shard_map/cross_forward/pallas_call | solution.py:238
  208.4 4.3 second_norm.1
  212.7 0.0 all-gather.2.cloned.1.call-done
  212.7 13.7 %ffn_forward.1 = (bf16[256,4096]{1,0:T(8,128)(2,1)}, f32[256,4096]{1,0:T(8,128)}, bf16[256,1024]{1,0:T(8,128)(2,1)}, f32[256,1024]{1,0:T(8,128)}, bf16[256,1024]{1,0:T(8,128)(2,1)}, /*index=5*/f32[8,1024]{1,0:T(8,128)}) custom-call(bf16[256,1024]{1,0:T(8,128)(2,1)} %get-tuple-element.64.low, f32[256,1024]{1,0:T(8,128)} %get-tuple-element.65.second, ...), custom_call_target="tpu_custom_call" | custom-call | flops 4294967296 | bytes 25165824 | tf_op jit(solution)/shard_map/ffn_forward/pallas_call | solution.py:303
  226.4 14.4 %ffn_backward.1 = (bf16[256,4096]{1,0:T(8,128)(2,1)}, f32[256,1024]{1,0:T(8,128)}, bf16[256,1024]{1,0:T(8,128)(2,1)}, bf16[256,1024]{1,0:T(8,128)(2,1)}, f32[8,1024]{1,0:T(8,128)}) custom-call(bf16[256,1024]{1,0:T(8,128)(2,1)} %get-tuple-element.67.go, f32[256,1024]{1,0:T(8,128)} %get-tuple-element.68.gts, f32[256,4096]{1,0:T(8,128)} %get-tuple-element.69.slope, ...), custom_call_target="tpu_custom_call" | custom-call | flops 4831838208 | bytes 27262976 | tf_op jit(solution)/shard_map/ffn_backward/pallas_call | solution.py:344
  240.8 11.9 %ffn_weights.1 = bf16[32,256,1024]{2,1,0:T(8,128)(2,1)} custom-call(bf16[256,4096]{1,0:T(8,128)(2,1)} %get-tuple-element.97.act, bf16[256,1024]{1,0:T(8,128)(2,1)} %get-tuple-element.67.go, bf16[256,1024]{1,0:T(8,128)(2,1)} %get-tuple-element.64.low, bf16[256,4096]{1,0:T(8,128)(2,1)} %get-tuple-element.98.gi), custom_call_target="tpu_custom_call" | custom-call | flops 4294967296 | bytes 23068672 | tf_op jit(solution)/shard_map/ffn_weights/pallas_call | solution.py:500
  252.7 0.0 reduce-scatter.2.cloned.1.call-update
  252.7 0.1 pad.12.clone
  252.8 26.3 %cross_backward.1 = (bf16[256,1024]{1,0:T(8,128)(2,1)}, bf16[2048,1024]{1,0:T(8,128)(2,1)}, bf16[2048,1024]{1,0:T(8,128)(2,1)}) custom-call(s32[1]{0:T(128)S(6)} %copy.54.length, bf16[256,1024]{1,0:T(8,128)(2,1)} %get-tuple-element.59.q, bf16[2048,1024]{1,0:T(8,128)(2,1)} %get-tuple-element.60.k, bf16[2048,1024]{1,0:T(8,128)(2,1)} %get-tuple-element.61.v, ...), custom_call_target="tpu_custom_call" | custom-call | flops 21474836480 | bytes 18874368 | tf_op jit(solution)/shard_map/cross_backward/pallas_call | solution.py:387
  279.1 9.9 %self_backward.1 = (f32[256,1024]{1,0:T(8,128)}, bf16[256,1024]{1,0:T(8,128)(2,1)}, bf16[256,1024]{1,0:T(8,128)(2,1)}, bf16[256,1024]{1,0:T(8,128)(2,1)}, bf16[256,1024]{1,0:T(8,128)(2,1)}, /*index=5*/f32[8,1024]{1,0:T(8,128)}) custom-call(s32[1]{0:T(128)S(6)} %copy.53.length, f32[256,1024]{1,0:T(8,128)} %get-tuple-element.71.gss, ...), custom_call_target="tpu_custom_call" | custom-call | flops 2147483648 | bytes 12582912 | tf_op jit(solution)/shard_map/self_backward/pallas_call | solution.py:443
  289.0 0.8 slice.86
  289.7 0.8 slice.87
  290.5 0.8 slice.88
  291.3 0.7 maximum_maximum_fusion.refs_8_
  292.0 8.4 %self_weights.1 = (bf16[16,160,1024]{2,1,0:T(8,128)(2,1)}, bf16[16,160,1024]{2,1,0:T(8,128)(2,1)}) custom-call(s32[1]{0:T(128)} %bitcast.9.me, bf16[256,1024]{1,0:T(8,128)(2,1)} %refs_4_.3, bf16[256,1024]{1,0:T(8,128)(2,1)} %get-tuple-element.82.gq.refs_1_, bf16[256,1024]{1,0:T(8,128)(2,1)} %refs_4_.3, bf16[256,1024]{1,0:T(8,128)(2,1)} %get-tuple-element.83.gk.refs_3_, ...), custom_call_target="tpu_custom_call" | custom-call | flops 2147483648 | bytes 20971520 | tf_op jit(solution)/shard_map/self_weights/pallas_call | solution.py:547
  300.4 17.1 %cross_weights.1 = (bf16[16,128,1024]{2,1,0:T(8,128)(2,1)}, bf16[16,128,1024]{2,1,0:T(8,128)(2,1)}) custom-call(s32[1]{0:T(128)} %bitcast.9.me, bf16[256,1024]{1,0:T(8,128)(2,1)} %get-tuple-element.87.refs_0_, bf16[256,1024]{1,0:T(8,128)(2,1)} %get-tuple-element.74.dcq.refs_1_, bf16[2048,1024]{1,0:T(8,128)(2,1)} %refs_4_.2, ...), custom_call_target="tpu_custom_call" | custom-call | flops 9663676416 | bytes 20971520 | tf_op jit(solution)/shard_map/cross_weights/pallas_call | solution.py:547
  317.5 192.6 %scatter_rows.1 = f32[288,1024]{1,0:T(8,128)} custom-call(bf16[16,128,1024]{2,1,0:T(8,128)(2,1)} %get-tuple-element.89.refs_0_, bf16[16,128,1024]{2,1,0:T(8,128)(2,1)} %get-tuple-element.90.refs_1_, bf16[16,160,1024]{2,1,0:T(8,128)(2,1)} %get-tuple-element.95.refs_2_, bf16[16,160,1024]{2,1,0:T(8,128)(2,1)} %get-tuple-element.96.refs_3_), custom_call_target="tpu_custom_call" | custom-call | tf_op jit(solution)/shard_map/scatter_rows/pallas_call | solution.py:733
  510.1 0.0 copy-start
  510.1 6.6 %tokens_grad.1 = f32[256,1024]{1,0:T(8,128)} custom-call(f32[256,1024]{1,0:T(8,128)} %get-tuple-element.81.gfs, bf16[256,1024]{1,0:T(8,128)(2,1)} %get-tuple-element.82.gq.refs_1_, bf16[256,1024]{1,0:T(8,128)(2,1)} %get-tuple-element.83.gk.refs_3_, bf16[256,1024]{1,0:T(8,128)(2,1)} %get-tuple-element.84.gv.refs_5_, bf16[32,288,1024]{2,1,0:T(8,128)(2,1)} %bitcast.36, ...), custom_call_target="tpu_custom_call" | custom-call | flops 1610612736 | bytes 10485760 | tf_op jit(solution)/shard_map/tokens_grad/pallas_call | solution.py:458
  516.8 0.0 copy-done
  516.8 0.5 slice_bitcast_fusion
  517.3 1.0 fusion
  518.3 13.8 %memory_grad.1 = f32[2048,1024]{1,0:T(8,128)} custom-call(bf16[2048,1024]{1,0:T(8,128)(2,1)} %get-tuple-element.85.dk.refs_3_, bf16[2048,1024]{1,0:T(8,128)(2,1)} %get-tuple-element.86.dv.refs_5_, bf16[32,288,1024]{2,1,0:T(8,128)(2,1)} %bitcast.39, bf16[32,288,1024]{2,1,0:T(8,128)(2,1)} %bitcast.40), custom_call_target="tpu_custom_call" | custom-call | flops 8589934592 | bytes 20971520 | tf_op jit(solution)/shard_map/memory_grad/pallas_call | solution.py:404
  532.1 0.0 reduce-scatter.2.cloned.1.call-done
  532.1 1.0 fusion.1
  533.1 0.8 pad_maximum_fusion
  533.9 1.8 slice.113
  (3 shorter events, 0.0 us)
Async XLA Ops:
  7.2 205.5 %all-gather.2.cloned.1.call-start = ((), (), s32[]{:S(2)}) async-start(), calls=%async_computation.1 | async-start | bytes 17301504 | tf_op jit(solution)/shard_map/all_gather | solution.py:756
  11.6 0.8 copy-start.1
  12.4 519.7 %reduce-scatter.2.cloned.1.call-start = ((), (), s32[]{:S(2)}) async-start(), calls=%async_computation.2 | async-start | bytes 17301504 | tf_op jit(solution)/shard_map/reduce_scatter | solution.py:809
  510.1 6.6 %copy-start = (f32[288,1024]{1,0:T(8,128)S(1)}, f32[288,1024]{1,0:T(8,128)}, u32[]{:S(2)}) copy-start(f32[288,1024]{1,0:T(8,128)} %scatter_rows.1) | copy-start | bytes 3538948
Sparse Core Ops, SparseCore 0:
  12.5 176.9 all-gather.1
  252.8 273.5 reduce-scatter.1
